TPU v7x, 32 devices: a whole 2x2x4 slice. The times are simulated.
32 devices in a mesh: dp: 8 (over z, x), narrow: 4 (over y, core).
Axes of the slice: x: 2, y: 2, z: 4, core: 2. Of those that a mesh axis runs over, the one named last changes fastest.
Arguments:
- view_maps: bfloat16 [2, 18816, 2048], P(None, ('dp', 'narrow')), may hold values from -33 to 33
- crop_maps: bfloat16 [2, 6912, 2048], P(None, ('dp', 'narrow')), may hold values from -33 to 33
- image_ids: int32 [2, 192], replicated, may hold values from 0 to 95
- w_reduce: bfloat16 [2048, 512], replicated, may hold values from -0.125 to 0.125
- gain_one: float32 [512], replicated, may hold values from 0.25 to 1.75
- shift_one: float32 [512], replicated, may hold values from -0.5 to 0.5
- w_spatial: bfloat16 [4608, 512], replicated, may hold values from -0.09375 to 0.09375
- gain_two: float32 [512], replicated, may hold values from 0.25 to 1.75
- shift_two: float32 [512], replicated, may hold values from -0.5 to 0.5
- w_expand: bfloat16 [512, 2048], replicated, may hold values from -0.25 to 0.25
- gain_three: float32 [2048], replicated, may hold values from 0.25 to 1.75
- shift_three: float32 [2048], replicated, may hold values from -0.5 to 0.5
- w_hidden: bfloat16 [2048, 2048], replicated, may hold values from -0.125 to 0.125
- gain_head: float32 [2048], replicated, may hold values from 0.25 to 1.75
- shift_head: float32 [2048], replicated, may hold values from -0.5 to 0.5
- w_embed: bfloat16 [2048, 128], replicated, may hold values from -0.125 to 0.125
Outputs:
- anchor_loss: float32 [2, 1152], P(None, ('dp', 'narrow'))
- grad_views: float32 [2, 18816, 2048], P(None, ('dp', 'narrow'))
- grad_crops: float32 [2, 6912, 2048], P(None, ('dp', 'narrow'))
- grad_w_reduce: float32 [2048, 512], P('dp')
- grad_gain_one: float32 [512], replicated
- grad_shift_one: float32 [512], replicated
- grad_w_spatial: float32 [4608, 512], P('dp')
- grad_gain_two: float32 [512], replicated
- grad_shift_two: float32 [512], replicated
- grad_w_expand: float32 [512, 2048], P('dp')
- grad_gain_three: float32 [2048], replicated
- grad_shift_three: float32 [2048], replicated
- grad_w_hidden: float32 [2048, 2048], P('dp')
- grad_gain_head: float32 [2048], replicated
- grad_shift_head: float32 [2048], replicated
- grad_w_embed: float32 [2048, 128], P('dp')
Inputs may be any that keep to these rules, and one draw needn't show every extreme that they name: image_ids[m, i] is the id of image i of micro-batch m; embeddings of micro-batch m whose images have equal ids are positives of each other.
All inputs are finite; a program needn't handle non-finite values.
Results may differ from a plain program's by a relative error of at most 0.022.
Values may be sent and summed in bfloat16 or wider, within the bound.
No kernel may reach another device: no remote copies, remote signals or barrier semaphores. Data moves between devices by JAX's collectives and lax.ppermute only.
A program may use at most 256 MiB of HBM per device.

v0:
```python
import jax
import jax.numpy as jnp
from jax import lax
from jax.sharding import PartitionSpec as P

VIEWS = 2
CROPS = 4
VSIDE = 7
CSIDE = 3


logit_divisor_tau = 0.1
epsilon = 1e-05


def combined_all(array, axis, combine):
    everything = jax.tree.map(lambda part: lax.all_gather(part, axis), array)
    initial = jax.tree.map(lambda part: part[0], everything)

    def step(k, so_far):
        return combine(so_far, jax.tree.map(lambda part: part[k], everything))

    return lax.fori_loop(1, lax.axis_size(axis), step, initial)


def silu_slope(values):
    sigma = jax.nn.sigmoid(values)
    return sigma * (1.0 + values * (1.0 - sigma))


def matmul(left, right):
    return jnp.dot(left, right, preferred_element_type=jnp.float32)


def matmul_left_t(left, right):
    return lax.dot_general(
        left, right, (((0,), (0,)), ((), ())), preferred_element_type=jnp.float32
    )


def matmul_right_t(left, right):
    return lax.dot_general(
        left, right, (((1,), (1,)), ((), ())), preferred_element_type=jnp.float32
    )


def spread_taps(hidden, map_side):
    padded = jnp.pad(hidden, ((0, 0), (1, 1), (1, 1), (0, 0)))
    pieces = [
        padded[:, tap_row : tap_row + map_side, tap_col : tap_col + map_side, :]
        for tap_row in range(3)
        for tap_col in range(3)
    ]
    return jnp.concatenate(pieces, axis=-1).reshape(-1, 9 * hidden.shape[-1])


def gather_taps(grad_cols, map_side, channels):
    tap_grid = grad_cols.reshape(-1, map_side, map_side, 9, channels)
    accum = jnp.zeros((tap_grid.shape[0], map_side + 2, map_side + 2, channels), jnp.float32)
    for tap_row in range(3):
        for tap_col in range(3):
            accum = accum + jnp.pad(
                tap_grid[:, :, :, 3 * tap_row + tap_col, :],
                ((0, 0), (tap_row, 2 - tap_row), (tap_col, 2 - tap_col), (0, 0)),
            )
    return accum[:, 1 : map_side + 1, 1 : map_side + 1, :].reshape(-1, channels)


def forward_norm(tensor, row_count):
    stacked = jnp.stack([jnp.sum(tensor, axis=1), jnp.sum(tensor * tensor, axis=1)], axis=1)
    totals = lax.psum(stacked, ("dp", "narrow"))
    means = totals[:, 0] / row_count
    variance = totals[:, 1] / row_count - means * means
    inv_std = lax.rsqrt(variance + epsilon)
    return ((tensor - means[:, None, :]) * inv_std[:, None, :], inv_std)


def backward_norm(slopes, normed, inv_std, gain_vec, row_count):
    stacked = jnp.stack([jnp.sum(slopes, axis=1), jnp.sum(slopes * normed, axis=1)], axis=1)
    totals = lax.psum(stacked, ("dp", "narrow"))
    grad_input = (
        gain_vec
        * inv_std[:, None, :]
        * (
            slopes
            - totals[:, 0][:, None, :] / row_count
            - normed * totals[:, 1][:, None, :] / row_count
        )
    )
    return (grad_input, jnp.sum(totals[:, 1], axis=0), jnp.sum(totals[:, 0], axis=0))


def combine_totals(earlier, later):
    highest = jnp.maximum(earlier[0], later[0])
    merged_sum = earlier[1] * jnp.exp(earlier[0] - highest) + later[1] * jnp.exp(later[0] - highest)
    return (highest, merged_sum, earlier[2] + later[2])


def body(
    view_maps,
    crop_maps,
    image_ids,
    w_reduce,
    gain_one,
    shift_one,
    w_spatial,
    gain_two,
    shift_two,
    w_expand,
    gain_three,
    shift_three,
    w_hidden,
    gain_head,
    shift_head,
    w_embed,
):
    micro_count = view_maps.shape[0]
    view_rows = view_maps.shape[1]
    crop_rows = crop_maps.shape[1]
    pixel_rows = view_rows + crop_rows
    channels = w_reduce.shape[0]
    mid_width = w_reduce.shape[1]
    hidden_width = w_hidden.shape[1]
    embedding_dimension = w_embed.shape[1]
    images_dev = view_rows // (VIEWS * VSIDE * VSIDE)
    local_anchor_rows = images_dev * (VIEWS + CROPS)
    data_size = lax.axis_size("dp")
    narrow_size = lax.axis_size("narrow")
    devices = data_size * narrow_size
    emb_total = local_anchor_rows * devices
    pixel_count = pixel_rows * devices
    data_index = lax.axis_index("dp")
    narrow_index = lax.axis_index("narrow")
    loss_scale = 1.0 / (micro_count * emb_total)
    views_per_image = 1
    anchor_rows = local_anchor_rows * narrow_size
    cand_rows = local_anchor_rows * data_size
    anchor_order = data_index * anchor_rows + jnp.arange(anchor_rows, dtype=jnp.int32)
    cand_order = jnp.arange(cand_rows, dtype=jnp.int32)
    cand_global = (
        cand_order // local_anchor_rows * narrow_size + narrow_index
    ) * local_anchor_rows + cand_order % local_anchor_rows
    self_mask = anchor_order[:, None] == cand_global[None, :]
    norm_grads = [
        jnp.zeros_like(gain_one),
        jnp.zeros_like(shift_one),
        jnp.zeros_like(gain_two),
        jnp.zeros_like(shift_two),
        jnp.zeros_like(gain_three),
        jnp.zeros_like(shift_three),
        jnp.zeros_like(gain_head),
        jnp.zeros_like(shift_head),
    ]
    weight_accum = None
    anchor_terms = []
    view_grads = []
    crop_grads = []
    for first_micro in range(0, micro_count, views_per_image):
        view_part = view_maps[first_micro : first_micro + views_per_image]
        crop_part = crop_maps[first_micro : first_micro + views_per_image]
        pixels = jnp.concatenate([view_part, crop_part], axis=1)
        pixel_flat = pixels.reshape(views_per_image * pixel_rows, channels)
        act_one = matmul(pixel_flat, w_reduce).reshape(views_per_image, pixel_rows, mid_width)
        normed_one, inv_one = forward_norm(act_one, pixel_count)
        pre_one = normed_one * gain_one + shift_one
        hid_one = jax.nn.silu(pre_one).astype(jnp.bfloat16)
        view_cols = spread_taps(hid_one[:, :view_rows].reshape(-1, VSIDE, VSIDE, mid_width), VSIDE)
        crop_cols = spread_taps(hid_one[:, view_rows:].reshape(-1, CSIDE, CSIDE, mid_width), CSIDE)
        tap_cols = jnp.concatenate(
            [
                view_cols.reshape(views_per_image, view_rows, 9 * mid_width),
                crop_cols.reshape(views_per_image, crop_rows, 9 * mid_width),
            ],
            axis=1,
        ).reshape(views_per_image * pixel_rows, 9 * mid_width)
        act_two = matmul(tap_cols, w_spatial).reshape(views_per_image, pixel_rows, mid_width)
        normed_two, inv_two = forward_norm(act_two, pixel_count)
        pre_two = normed_two * gain_two + shift_two
        hid_two = jax.nn.silu(pre_two).astype(jnp.bfloat16)
        hid_two_flat = hid_two.reshape(views_per_image * pixel_rows, mid_width)
        act_three = matmul(hid_two_flat, w_expand).reshape(views_per_image, pixel_rows, channels)
        normed_three, inv_three = forward_norm(act_three, pixel_count)
        resid = normed_three * gain_three + shift_three + pixels.astype(jnp.float32)
        block_out = jax.nn.silu(resid)
        pooled_views = jnp.mean(
            block_out[:, :view_rows].reshape(
                views_per_image, images_dev, VIEWS, VSIDE * VSIDE, channels
            ),
            axis=3,
        )
        pooled_crops = jnp.mean(
            block_out[:, view_rows:].reshape(
                views_per_image, images_dev, CROPS, CSIDE * CSIDE, channels
            ),
            axis=3,
        )
        pooled = (
            jnp.concatenate([pooled_views, pooled_crops], axis=2)
            .reshape(views_per_image * local_anchor_rows, channels)
            .astype(jnp.bfloat16)
        )
        head_act = matmul(pooled, w_hidden).reshape(
            views_per_image, local_anchor_rows, hidden_width
        )
        normed_head, inv_head = forward_norm(head_act, emb_total)
        pre_head = normed_head * gain_head + shift_head
        head_hid = jax.nn.silu(pre_head).astype(jnp.bfloat16)
        head_flat = head_hid.reshape(views_per_image * local_anchor_rows, hidden_width)
        embedding = matmul(head_flat, w_embed).reshape(
            views_per_image, local_anchor_rows, embedding_dimension
        )
        inv_len = lax.rsqrt(jnp.sum(embedding * embedding, axis=2, keepdims=True) + 1e-06)
        unit_length_features = embedding * inv_len
        unit_low = unit_length_features.astype(jnp.bfloat16)
        anchors = lax.all_gather(unit_low, "narrow", axis=1, tiled=True)
        candidates = lax.all_gather(unit_low, "dp", axis=1, tiled=True)
        cosine_logit_matrix = (
            jnp.einsum("gae,gce->gac", anchors, candidates, preferred_element_type=jnp.float32)
            / logit_divisor_tau
        )
        ids_emb = jnp.repeat(
            image_ids[first_micro : first_micro + views_per_image], VIEWS + CROPS, axis=1
        )
        anchor_ids = lax.dynamic_slice_in_dim(
            ids_emb, data_index * anchor_rows, anchor_rows, axis=1
        )
        cand_ids = lax.dynamic_index_in_dim(
            ids_emb.reshape(views_per_image, data_size, narrow_size, local_anchor_rows),
            narrow_index,
            axis=2,
            keepdims=False,
        ).reshape(views_per_image, cand_rows)
        counts = (
            jnp.sum((anchor_ids[:, :, None] == ids_emb[:, None, :]).astype(jnp.float32), axis=2)
            - 1.0
        )
        positive = (anchor_ids[:, :, None] == cand_ids[:, None, :]) & jnp.logical_not(self_mask)
        diagonal_excluded = jnp.where(self_mask, -1e30, cosine_logit_matrix)
        tile_max = jnp.max(diagonal_excluded, axis=2)
        tile_sum = jnp.sum(jnp.exp(diagonal_excluded - tile_max[:, :, None]), axis=2)
        tile_pos = jnp.sum(jnp.where(positive, cosine_logit_matrix, 0.0), axis=2)
        merged_max, merged_sum, merged_pos = combined_all(
            (tile_max, tile_sum, tile_pos), "narrow", combine_totals
        )
        log_total = merged_max + jnp.log(merged_sum)
        per_anchor = log_total - merged_pos / counts
        anchor_terms.append(
            lax.dynamic_slice_in_dim(
                per_anchor, narrow_index * local_anchor_rows, local_anchor_rows, axis=1
            )
        )
        probs = jnp.exp(diagonal_excluded - log_total[:, :, None])
        grad_tile = (
            (probs - positive.astype(jnp.float32) / counts[:, :, None]) * loss_scale
        ).astype(jnp.bfloat16)
        grad_anchor = (
            jnp.einsum("gac,gce->gae", grad_tile, candidates, preferred_element_type=jnp.float32)
            / logit_divisor_tau
        )
        anchor_part = lax.psum_scatter(
            grad_anchor.astype(jnp.bfloat16), "narrow", scatter_dimension=1, tiled=True
        ).astype(jnp.float32)
        loss_contribution = jnp.einsum(
            "gac,gae->cge", grad_tile, anchors, preferred_element_type=jnp.float32
        )
        cand_part = lax.psum_scatter(
            loss_contribution.reshape(
                local_anchor_rows * lax.axis_size("dp"), views_per_image * embedding_dimension
            )
            / logit_divisor_tau,
            "dp",
            scatter_dimension=0,
            tiled=True,
        )
        grad_unit = anchor_part + jnp.transpose(
            cand_part.reshape(local_anchor_rows, views_per_image, embedding_dimension), (1, 0, 2)
        )
        grad_embed = (
            inv_len
            * (
                grad_unit
                - unit_length_features
                * jnp.sum(unit_length_features * grad_unit, axis=2, keepdims=True)
            )
        ).astype(jnp.bfloat16)
        grad_embed_flat = grad_embed.reshape(
            views_per_image * local_anchor_rows, embedding_dimension
        )
        grad_w_embed = matmul_left_t(head_flat, grad_embed_flat)
        grad_head_hid = matmul_right_t(grad_embed_flat, w_embed).reshape(
            views_per_image, local_anchor_rows, hidden_width
        )
        grad_head_act, gain_grad, shift_grad = backward_norm(
            grad_head_hid * silu_slope(pre_head), normed_head, inv_head, gain_head, emb_total
        )
        norm_grads[6] = norm_grads[6] + gain_grad
        norm_grads[7] = norm_grads[7] + shift_grad
        grad_head_flat = grad_head_act.astype(jnp.bfloat16).reshape(
            views_per_image * local_anchor_rows, hidden_width
        )
        grad_w_hidden = matmul_left_t(pooled, grad_head_flat)
        grad_pooled = matmul_right_t(grad_head_flat, w_hidden).reshape(
            views_per_image, images_dev, VIEWS + CROPS, channels
        )
        view_back = jnp.broadcast_to(
            grad_pooled[:, :, :VIEWS, None, :] / (VSIDE * VSIDE),
            (views_per_image, images_dev, VIEWS, VSIDE * VSIDE, channels),
        ).reshape(views_per_image, view_rows, channels)
        crop_back = jnp.broadcast_to(
            grad_pooled[:, :, VIEWS:, None, :] / (CSIDE * CSIDE),
            (views_per_image, images_dev, CROPS, CSIDE * CSIDE, channels),
        ).reshape(views_per_image, crop_rows, channels)
        grad_resid = jnp.concatenate([view_back, crop_back], axis=1) * silu_slope(resid)
        grad_act_three, gain_grad, shift_grad = backward_norm(
            grad_resid, normed_three, inv_three, gain_three, pixel_count
        )
        norm_grads[4] = norm_grads[4] + gain_grad
        norm_grads[5] = norm_grads[5] + shift_grad
        grad_three_flat = grad_act_three.astype(jnp.bfloat16).reshape(
            views_per_image * pixel_rows, channels
        )
        grad_w_expand = matmul_left_t(hid_two_flat, grad_three_flat)
        grad_hid_two = matmul_right_t(grad_three_flat, w_expand).reshape(
            views_per_image, pixel_rows, mid_width
        )
        grad_act_two, gain_grad, shift_grad = backward_norm(
            grad_hid_two * silu_slope(pre_two), normed_two, inv_two, gain_two, pixel_count
        )
        norm_grads[2] = norm_grads[2] + gain_grad
        norm_grads[3] = norm_grads[3] + shift_grad
        grad_two_flat = grad_act_two.astype(jnp.bfloat16).reshape(
            views_per_image * pixel_rows, mid_width
        )
        grad_w_spatial = matmul_left_t(tap_cols, grad_two_flat)
        grad_cols = matmul_right_t(grad_two_flat, w_spatial).reshape(
            views_per_image, pixel_rows, 9 * mid_width
        )
        grad_hid_view = gather_taps(
            grad_cols[:, :view_rows].reshape(-1, 9 * mid_width), VSIDE, mid_width
        )
        grad_hid_crop = gather_taps(
            grad_cols[:, view_rows:].reshape(-1, 9 * mid_width), CSIDE, mid_width
        )
        grad_hid_one = jnp.concatenate(
            [
                grad_hid_view.reshape(views_per_image, view_rows, mid_width),
                grad_hid_crop.reshape(views_per_image, crop_rows, mid_width),
            ],
            axis=1,
        )
        grad_act_one, gain_grad, shift_grad = backward_norm(
            grad_hid_one * silu_slope(pre_one), normed_one, inv_one, gain_one, pixel_count
        )
        norm_grads[0] = norm_grads[0] + gain_grad
        norm_grads[1] = norm_grads[1] + shift_grad
        grad_one_flat = grad_act_one.astype(jnp.bfloat16).reshape(
            views_per_image * pixel_rows, mid_width
        )
        grad_w_reduce = matmul_left_t(pixel_flat, grad_one_flat)
        grad_pixels = grad_resid + matmul_right_t(grad_one_flat, w_reduce).reshape(
            views_per_image, pixel_rows, channels
        )
        view_grads.append(grad_pixels[:, :view_rows])
        crop_grads.append(grad_pixels[:, view_rows:])
        fresh = (grad_w_reduce, grad_w_spatial, grad_w_expand, grad_w_hidden, grad_w_embed)
        if weight_accum is None:
            weight_accum = tuple(fresh)
        else:
            weight_accum = tuple((older + newer for older, newer in zip(weight_accum, fresh)))
    accumulated_total = (
        lax.psum_scatter(weight_accum[0], "dp", scatter_dimension=0, tiled=True),
        lax.psum_scatter(weight_accum[1], "dp", scatter_dimension=0, tiled=True),
        lax.psum_scatter(weight_accum[2], "dp", scatter_dimension=0, tiled=True),
        lax.psum_scatter(weight_accum[3], "dp", scatter_dimension=0, tiled=True),
        lax.psum_scatter(weight_accum[4], "dp", scatter_dimension=0, tiled=True),
    )
    reduced = (
        lax.psum(accumulated_total[0].astype(jnp.bfloat16), "narrow").astype(jnp.float32),
        lax.psum(accumulated_total[1].astype(jnp.bfloat16), "narrow").astype(jnp.float32),
        lax.psum(accumulated_total[2].astype(jnp.bfloat16), "narrow").astype(jnp.float32),
        lax.psum(accumulated_total[3].astype(jnp.bfloat16), "narrow").astype(jnp.float32),
        lax.psum(accumulated_total[4].astype(jnp.bfloat16), "narrow").astype(jnp.float32),
    )
    anchor_loss = jnp.concatenate(anchor_terms, axis=0)
    grad_views = jnp.concatenate(view_grads, axis=0)
    grad_crops = jnp.concatenate(crop_grads, axis=0)
    return (
        anchor_loss,
        grad_views,
        grad_crops,
        reduced[0],
        norm_grads[0],
        norm_grads[1],
        reduced[1],
        norm_grads[2],
        norm_grads[3],
        reduced[2],
        norm_grads[4],
        norm_grads[5],
        reduced[3],
        norm_grads[6],
        norm_grads[7],
        reduced[4],
    )


def solution(mesh):
    placed = (
        P(None, ("dp", "narrow"), None),
        P(None, ("dp", "narrow"), None),
        P(),
        P(),
        P(),
        P(),
        P(),
        P(),
        P(),
        P(),
        P(),
        P(),
        P(),
        P(),
        P(),
        P(),
    )
    return jax.shard_map(
        body,
        mesh=mesh,
        in_specs=placed,
        out_specs=(
            P(None, ("dp", "narrow")),
            P(None, ("dp", "narrow"), None),
            P(None, ("dp", "narrow"), None),
            P("dp", None),
            P(),
            P(),
            P("dp", None),
            P(),
            P(),
            P("dp", None),
            P(),
            P(),
            P("dp", None),
            P(),
            P(),
            P("dp", None),
        ),
        check_vma=False,
    )
```

profile of v0, /device:TPU:0, one launch (start us, length us, event | category | flops | bytes accessed | tf_op | source)
XLA Modules:
  0.0 1731.9 jit_solution(5713409424978603291)
XLA Ops:
  8.4 10.2 fusion.112
  35.7 42.3 %all-reduce.61 = (f32[1,2,512]{2,1,0:T(2,128)S(1)}, f32[1,2,512]{2,1,0:T(2,128)S(1)}) all-reduce(f32[1,2,512]{2,1,0:T(2,128)S(1)} %pad_maximum_fusion.12, f32[1,2,512]{2,1,0:T(2,128)S(1)} %pad_maximum_fusion.14), channel_id=1, replica_groups=mesh['dp'=8,'narrow'=4] {'dp','narrow'}, use_global_device_ids=true, to_apply=%region_2.3 | all-reduce | flops 2048 | bytes 16384 | tf_op jit(solution)/shard_map/psum | solution.py:71
  90.5 4.2 pad_slice_fusion.24
  160.7 5.8 pad_slice_fusion
  194.5 10.4 fusion.100
  206.3 8.3 fusion.98
  214.6 40.2 %all-reduce.60 = (f32[1,2,512]{2,1,0:T(2,128)S(1)}, f32[1,2,512]{2,1,0:T(2,128)S(1)}) all-reduce(f32[1,2,512]{2,1,0:T(2,128)S(1)} %pad_maximum_fusion.13, f32[1,2,512]{2,1,0:T(2,128)S(1)} %pad_maximum_fusion.15), channel_id=1, replica_groups=mesh['dp'=8,'narrow'=4] {'dp','narrow'}, use_global_device_ids=true, to_apply=%region_5.6 | all-reduce | flops 2048 | bytes 16384 | tf_op jit(solution)/shard_map/psum | solution.py:71
  254.9 6.4 fusion.93
  261.4 4.9 fusion.92
  266.4 40.5 %all-reduce.59 = (f32[1,2,2048]{2,1,0:T(2,128)S(1)}, f32[1,2,2048]{2,1,0:T(2,128)S(1)}) all-reduce(f32[1,2,2048]{2,1,0:T(2,128)S(1)} %pad_maximum_fusion.4, f32[1,2,2048]{2,1,0:T(2,128)S(1)} %pad_maximum_fusion.6), channel_id=1, replica_groups=mesh['dp'=8,'narrow'=4] {'dp','narrow'}, use_global_device_ids=true, to_apply=%region_8.9 | all-reduce | flops 8192 | bytes 65536 | tf_op jit(solution)/shard_map/psum | solution.py:71
  307.0 9.1 multiply_bitcast_fusion
  324.0 4.7 reshape.1263
  338.7 4.7 reshape.1255
  352.6 5.1 fusion.105
  357.7 5.7 fusion.104
  363.5 40.5 %all-reduce.58 = (f32[1,2,2048]{2,1,0:T(2,128)S(1)}, f32[1,2,2048]{2,1,0:T(2,128)S(1)}) all-reduce(f32[1,2,2048]{2,1,0:T(2,128)S(1)} %pad_maximum_fusion.5, f32[1,2,2048]{2,1,0:T(2,128)S(1)} %pad_maximum_fusion.7), channel_id=1, replica_groups=mesh['dp'=8,'narrow'=4] {'dp','narrow'}, use_global_device_ids=true, to_apply=%region_13.14 | all-reduce | flops 8192 | bytes 65536 | tf_op jit(solution)/shard_map/psum | solution.py:71
  407.0 6.0 all-gather.12
  412.9 30.5 %all-gather.13 = bf16[8,36,128]{2,1,0:T(8,128)(2,1)S(1)} all-gather(bf16[1,36,128]{2,1,0:T(8,128)(2,1)S(1)} %fusion.53), channel_id=8, replica_groups=mesh['dp'=8,'narrow'=4] {'dp'}, dimensions={0}, use_global_device_ids=true | all-gather | bytes 82944 | tf_op jit(solution)/shard_map/all_gather | solution.py:216
  443.9 5.7 all-gather.10
  449.6 32.5 %all-gather.11 = bf16[8,36,128]{2,1,0:T(8,128)(2,1)} all-gather(bf16[1,36,128]{2,1,0:T(8,128)(2,1)S(1)} %fusion.52), channel_id=3, replica_groups=mesh['dp'=8,'narrow'=4] {'dp'}, dimensions={0}, use_global_device_ids=true | all-gather | bytes 82944 | tf_op jit(solution)/shard_map/all_gather | solution.py:216
  513.8 11.4 all-reduce.62
  544.4 3.9 while.38
  555.5 9.3 fusion.107
  575.6 23.2 %fusion.106 = (f32[48,128]{1,0:T(8,128)S(1)}, f32[48,128]{1,0:T(8,128)S(1)}) fusion(f32[288,128]{1,0:T(8,128)} %fusion.24, f32[288,128]{1,0:T(8,128)} %fusion.25), kind=kCustom, calls=%all-reduce-scatter.4 | all-reduce-scatter fusion | flops 98305 | bytes 344576
  631.6 37.9 %all-reduce.57 = (f32[1,2,2048]{2,1,0:T(2,128)S(1)}, f32[1,2,2048]{2,1,0:T(2,128)S(1)}) all-reduce(f32[1,2,2048]{2,1,0:T(2,128)S(1)} %pad_maximum_fusion.10, f32[1,2,2048]{2,1,0:T(2,128)S(1)} %pad_maximum_fusion.8), channel_id=1, replica_groups=mesh['dp'=8,'narrow'=4] {'dp','narrow'}, use_global_device_ids=true, to_apply=%region_62.63 | all-reduce | flops 8192 | bytes 65536 | tf_op jit(solution)/shard_map/psum | solution.py:80
  672.1 6.2 fusion.15
  680.0 6.1 fusion.18
  700.6 4.7 broadcast_in_dim.66
  708.3 4.7 broadcast_in_dim.62
  713.0 17.9 %fusion.90 = (f32[2048]{0:T(1024)S(1)}, f32[2048]{0:T(1024)S(1)}, f32[804,2048]{1,0:T(8,128)}, f32[2048]{0:T(1024)S(1)}, f32[2048]{0:T(1024)S(1)}, /*index=5*/f32[804,2048]{1,0:T(8,128)}) fusion(f32[2048]{0:T(1024)S(1)} %bitcast.514, f32[804,2048]{1,0:T(8,128)} %get-tuple-element.838, f32[2048]{0:T(1024)S(1)} %bitcast.528, ...), kind=kLoop, calls=%fused_computation.416 | loop fusion | flops 69148672 | bytes 46186496 | tf_op jit(solution)/shard_map/reduce_sum | solution.py:79
  731.0 42.4 %all-reduce.56 = (f32[1,2,2048]{2,1,0:T(2,128)S(1)}, f32[1,2,2048]{2,1,0:T(2,128)S(1)}) all-reduce(f32[1,2,2048]{2,1,0:T(2,128)S(1)} %pad_maximum_fusion.11, f32[1,2,2048]{2,1,0:T(2,128)S(1)} %pad_maximum_fusion.9), channel_id=1, replica_groups=mesh['dp'=8,'narrow'=4] {'dp','narrow'}, use_global_device_ids=true, to_apply=%region_65.66 | all-reduce | flops 8192 | bytes 65536 | tf_op jit(solution)/shard_map/psum | solution.py:80
  774.1 8.5 multiply_convert_fusion.1
  782.7 6.3 fusion.95
  789.0 4.6 fusion.87
  797.2 6.1 fusion.97
  803.4 38.8 %all-reduce.55 = (f32[1,2,512]{2,1,0:T(2,128)S(1)}, f32[1,2,512]{2,1,0:T(2,128)S(1)}) all-reduce(f32[1,2,512]{2,1,0:T(2,128)S(1)} %pad_maximum_fusion.18, f32[1,2,512]{2,1,0:T(2,128)S(1)} %pad_maximum_fusion.16), channel_id=1, replica_groups=mesh['dp'=8,'narrow'=4] {'dp','narrow'}, use_global_device_ids=true, to_apply=%region_68.69 | all-reduce | flops 2048 | bytes 16384 | tf_op jit(solution)/shard_map/psum | solution.py:80
  845.1 6.3 convolution_bitcast_fusion
  851.4 5.2 copy-done.2
  858.9 9.1 slice.641
  869.8 7.6 convolution_add_fusion.2
  877.4 5.8 reshape_reshape.11
  883.2 14.1 reshape_reshape.10
  900.2 9.8 convolution_bitcast_fusion.1
  910.0 32.3 %fusion.109 = (f32[12,7,7,1,512]{4,3,2,1,0:T(1,128)S(1)}, f32[12,7,7,1,512]{4,3,2,1,0:T(1,128)}, f32[12,7,7,1,512]{4,3,2,1,0:T(1,128)}, f32[12,7,7,1,512]{4,3,2,...) fusion(f32[12,7,7,9,512]{4,3,2,1,0:T(8,128)} %reshape_reshape.10), kind=kLoop, calls=%fused_computation.433 | loop fusion | bytes 21676032 | tf_op jit(solution)/shard_map/slice | solution.py:63
  942.3 14.9 fusion.111
  957.2 4.5 slice.619
  961.7 9.1 slice.608
  981.9 5.9 reshape_reshape.9
  987.8 14.7 fusion.110
  1004.5 14.0 reshape_reshape.8
  1018.5 32.1 %fusion.108 = (f32[12,7,7,1,512]{4,3,2,1,0:T(1,128)S(1)}, f32[12,7,7,1,512]{4,3,2,1,0:T(1,128)}, f32[12,7,7,1,512]{4,3,2,1,0:T(1,128)}, f32[12,7,7,1,512]{4,3,2,...) fusion(f32[12,7,7,9,512]{4,3,2,1,0:T(8,128)} %reshape_reshape.8), kind=kLoop, calls=%fused_computation.432 | loop fusion | bytes 21676032 | tf_op jit(solution)/shard_map/slice | solution.py:63
  1059.7 4.7 fusion.94
  1064.4 41.6 %all-reduce.54 = (f32[1,2,512]{2,1,0:T(2,128)S(1)}, f32[1,2,512]{2,1,0:T(2,128)S(1)}) all-reduce(f32[1,2,512]{2,1,0:T(2,128)S(1)} %pad_maximum_fusion.19, f32[1,2,512]{2,1,0:T(2,128)S(1)} %pad_maximum_fusion.17), channel_id=1, replica_groups=mesh['dp'=8,'narrow'=4] {'dp','narrow'}, use_global_device_ids=true, to_apply=%region_71.72 | all-reduce | flops 2048 | bytes 16384 | tf_op jit(solution)/shard_map/psum | solution.py:80
  1113.8 4.6 convolution_add_fusion.3
  1119.5 7.5 fusion.13
  1127.0 9.9 convolution_add_fusion.1
  1140.3 8.3 convolution_add_fusion
  1150.3 7.8 add_bitcast_fusion
  1161.4 44.5 %reduce-scatter.16.cloned.1.call-done = f32[256,512]{1,0:T(8,128)} async-done(((f32[2048,512]{1,0:T(8,128)}), f32[256,512]{1,0:T(8,128)}) %reduce-scatter.16.cloned.1.call-update) | async-done | bytes 524304 | tf_op jit(solution)/shard_map/reduce_scatter | solution.py:371
  1207.7 165.9 %reduce-scatter.18.cloned.1.call-done = f32[576,512]{1,0:T(8,128)} async-done(((f32[4608,512]{1,0:T(8,128)}), f32[576,512]{1,0:T(8,128)}) %reduce-scatter.18.cloned.1.call-update) | async-done | bytes 1179664 | tf_op jit(solution)/shard_map/reduce_scatter | solution.py:372
  1375.8 283.9 %reduce-scatter.22.cloned.1.call-done = f32[256,2048]{1,0:T(8,128)} async-done(((f32[2048,2048]{1,0:T(8,128)}), f32[256,2048]{1,0:T(8,128)}) %reduce-scatter.22.cloned.1.call-update) | async-done | bytes 2097168 | tf_op jit(solution)/shard_map/reduce_scatter | solution.py:374
  1662.5 4.8 add_bitcast_fusion.1
  1681.8 12.8 copy.598
  1696.7 20.0 %all-reduce.68.cloned.1.call-done = (bf16[256,512]{1,0:T(8,128)(2,1)}, bf16[576,512]{1,0:T(8,128)(2,1)}, bf16[64,2048]{1,0:T(8,128)(2,1)}, bf16[256,2048]{1,0:T(8,128)(2,1)}, bf16[256,128]{1,0:T(8,128)(2,1)}) async-done(((bf16[256,512]{1,0:T(8,128)(2,1)}, bf16[576,512]{1,0:T(8,128)(2,1)}, bf16[64,2048]{1,0:T(8,128)(2,1)}, bf16[256,2048]{1,0:T(8,128)(2,1)}, bf16[256,128]{1,0:T(8,128)(2,1)}), ...) | async-done | bytes 2228240 | tf_op jit(solution)/shard_map/psum | solution.py:378
  (726 shorter events, 369.3 us)
Async XLA Ops:
  7.2 247.7 %copy-start = (bf16[512,2048]{1,0:T(8,128)(2,1)S(1)}, bf16[512,2048]{1,0:T(8,128)(2,1)}, u32[]{:S(2)}) copy-start(bf16[512,2048]{1,0:T(8,128)(2,1)} %param.29) | copy-start | bytes 6291460
  7.2 1150.9 %reduce-scatter.24.cloned.1.call-start = ((), (), s32[]{:S(2)}) async-start(), calls=%async_computation.9 | async-start | bytes 1179648 | tf_op jit(solution)/shard_map/reduce_scatter | solution.py:375
  20.1 8.7 copy-start.33
  32.6 45.5 %copy-start.153 = (f32[512]{0:T(512)S(1)}, f32[512]{0:T(512)}, u32[]{:S(2)}) copy-start(f32[512]{0:T(512)} %param.24) | copy-start | bytes 6148
  32.6 45.5 %copy-start.164 = (f32[512]{0:T(512)S(1)}, f32[512]{0:T(512)}, u32[]{:S(2)}) copy-start(f32[512]{0:T(512)} %param.25) | copy-start | bytes 6148
  119.1 12.9 copy-start.66
  194.1 12.1 slice-start.7
  194.5 10.5 copy-start.119
  194.5 10.5 copy-start.40
  194.5 10.5 copy-start.39
  194.5 11.8 slice-start.8
  206.3 48.6 %copy-start.125 = (f32[512]{0:T(512)S(1)}, f32[512]{0:T(512)}, u32[]{:S(2)}) copy-start(f32[512]{0:T(512)} %param.27) | copy-start | bytes 6148
  206.3 48.6 %copy-start.139 = (f32[512]{0:T(512)S(1)}, f32[512]{0:T(512)}, u32[]{:S(2)}) copy-start(f32[512]{0:T(512)} %param.28) | copy-start | bytes 6148
  261.4 45.6 %copy-start.117 = (f32[2048]{0:T(1024)S(1)}, f32[2048]{0:T(1024)}, u32[]{:S(2)}) copy-start(f32[2048]{0:T(1024)} %param.30) | copy-start | bytes 24580
  261.4 45.6 %copy-start.144 = (f32[2048]{0:T(1024)S(1)}, f32[2048]{0:T(1024)}, u32[]{:S(2)}) copy-start(f32[2048]{0:T(1024)} %param.31) | copy-start | bytes 24580
  306.9 9.2 copy-start.92
  306.9 9.2 copy-start.101
  307.0 9.2 copy-start.90
  307.0 9.2 copy-start.99
  357.7 46.4 %copy-start.141 = (f32[2048]{0:T(1024)S(1)}, f32[2048]{0:T(1024)}, u32[]{:S(2)}) copy-start(f32[2048]{0:T(1024)} %param.33) | copy-start | bytes 24580
  363.4 118.7 %copy-start.176 = (s32[2,192]{1,0:T(2,128)S(1)}, s32[2,192]{1,0:T(2,128)}, u32[]{:S(2)}) copy-start(s32[2,192]{1,0:T(2,128)} %param.22) | copy-start | bytes 4612
  404.0 39.5 %copy-start.51 = (bf16[2048,128]{1,0:T(8,128)(2,1)S(1)}, bf16[2048,128]{1,0:T(8,128)(2,1)}, u32[]{:S(2)}) copy-start(bf16[2048,128]{1,0:T(8,128)(2,1)} %param.35) | copy-start | bytes 1572868
  404.0 39.8 %copy-start.111 = (f32[1,1,2048]{2,1,0:T(1,128)}, f32[1,1,2048]{2,1,0:T(1,128)S(1)}, u32[]{:S(2)}) copy-start(f32[1,1,2048]{2,1,0:T(1,128)S(1)} %get-tuple-element.789) | copy-start | bytes 24580
  404.0 39.9 %copy-start.97 = (f32[1,1,2048]{2,1,0:T(1,128)}, f32[1,1,2048]{2,1,0:T(1,128)S(1)}, u32[]{:S(2)}) copy-start(f32[1,1,2048]{2,1,0:T(1,128)S(1)} %get-tuple-element.790) | copy-start | bytes 24580
  404.1 39.8 %copy-start.109 = (f32[1,1,2048]{2,1,0:T(1,128)}, f32[1,1,2048]{2,1,0:T(1,128)S(1)}, u32[]{:S(2)}) copy-start(f32[1,1,2048]{2,1,0:T(1,128)S(1)} %get-tuple-element.787) | copy-start | bytes 24580
  404.1 39.8 %copy-start.95 = (f32[1,1,2048]{2,1,0:T(1,128)}, f32[1,1,2048]{2,1,0:T(1,128)S(1)}, u32[]{:S(2)}) copy-start(f32[1,1,2048]{2,1,0:T(1,128)S(1)} %get-tuple-element.788) | copy-start | bytes 24580
  405.3 38.4 %copy-start.60 = (bf16[36,2048]{1,0:T(8,128)(2,1)}, bf16[36,2048]{1,0:T(8,128)(2,1)S(1)}, u32[]{:S(2)}) copy-start(bf16[36,2048]{1,0:T(8,128)(2,1)S(1)} %get-tuple-element.786) | copy-start | bytes 442372
  405.4 38.4 %copy-start.62 = (bf16[36,2048]{1,0:T(8,128)(2,1)}, bf16[36,2048]{1,0:T(8,128)(2,1)S(1)}, u32[]{:S(2)}) copy-start(bf16[36,2048]{1,0:T(8,128)(2,1)S(1)} %get-tuple-element.785) | copy-start | bytes 442372
  406.9 37.0 %copy-start.87 = (f32[36,128]{1,0:T(8,128)}, f32[36,128]{1,0:T(8,128)S(1)}, u32[]{:S(2)}) copy-start(f32[36,128]{1,0:T(8,128)S(1)} %get-tuple-element.847) | copy-start | bytes 55300
  406.9 36.6 %copy-start.167 = (f32[36]{0:T(128)}, f32[36]{0:T(128)S(1)}, u32[]{:S(2)}) copy-start(f32[36]{0:T(128)S(1)} %add_rsqrt_fusion.8) | copy-start | bytes 436
  443.8 39.8 %copy-start.166 = (f32[36]{0:T(128)}, f32[36]{0:T(128)S(1)}, u32[]{:S(2)}) copy-start(f32[36]{0:T(128)S(1)} %add_rsqrt_fusion.9) | copy-start | bytes 436
  502.5 47.8 %copy-start.75 = (f32[144,288]{1,0:T(8,128)}, f32[144,288]{1,0:T(8,128)S(1)}, u32[]{:S(2)}) copy-start(f32[144,288]{1,0:T(8,128)S(1)} %get-tuple-element.848) | copy-start | bytes 497668
  566.1 47.1 %collective-permute-start = (bf16[36,128]{1,0:T(8,128)(2,1)}, bf16[36,128]{1,0:T(8,128)(2,1)}, u32[]{:S(2)}, u32[]{:S(2)}) collective-permute-start(bf16[36,128]{1,0:T(8,128)(2,1)} %slice.668), channel_id=1, source_target_pairs={{0,1},{1,2},{2,3},{4,5},{5,6},{6,7},{8,9},{9,10},{10,11},{12,13},{... | collective-permute-start | bytes 27656
  569.3 49.1 %collective-permute-start.3 = (bf16[36,128]{1,0:T(8,128)(2,1)}, bf16[36,128]{1,0:T(8,128)(2,1)}, u32[]{:S(2)}, u32[]{:S(2)}) collective-permute-start(bf16[36,128]{1,0:T(8,128)(2,1)} %slice.670), channel_id=1, source_target_pairs={{0,1},{1,2},{2,3},{4,5},{5,6},{6,7},{8,9},{9,10},{10,11},{12,13},{... | collective-permute-start | bytes 27656
  573.9 55.7 %copy-start.96 = (f32[1,1,2048]{2,1,0:T(1,128)S(1)}, f32[1,1,2048]{2,1,0:T(1,128)}, u32[]{:S(2)}) copy-start(f32[1,1,2048]{2,1,0:T(1,128)} %copy-done.95) | copy-start | bytes 24580
  573.9 55.7 %copy-start.110 = (f32[1,1,2048]{2,1,0:T(1,128)S(1)}, f32[1,1,2048]{2,1,0:T(1,128)}, u32[]{:S(2)}) copy-start(f32[1,1,2048]{2,1,0:T(1,128)} %copy-done.109) | copy-start | bytes 24580
  573.9 55.7 %copy-start.142 = (f32[2048]{0:T(1024)S(1)}, f32[2048]{0:T(1024)}, u32[]{:S(2)}) copy-start(f32[2048]{0:T(1024)} %param.33) | copy-start | bytes 24580
  598.9 21.6 %collective-permute-start.4 = (f32[48,128]{1,0:T(8,128)S(1)}, f32[48,128]{1,0:T(8,128)}, u32[]{:S(2)}, u32[]{:S(2)}) collective-permute-start(f32[48,128]{1,0:T(8,128)S(1)} %get-tuple-element.682), channel_id=1, source_target_pairs={{0,4},{4,8},{8,12},{12,16},{16,20},{20,24},{24,28},{1,5},{5,9},{9,... | collective-permute-start | bytes 73736
  600.8 19.1 %collective-permute-start.5 = (f32[36,128]{1,0:T(8,128)S(1)}, f32[36,128]{1,0:T(8,128)S(1)}, u32[]{:S(2)}, u32[]{:S(2)}) collective-permute-start(f32[36,128]{1,0:T(8,128)S(1)} %slice.671), channel_id=1, source_target_pairs={{0,8},{4,12},{8,16},{12,20},{16,24},{20,28},{1,9},{5,13},{9,17},{1... | collective-permute-start | bytes 55304
  602.0 21.9 %collective-permute-start.1 = (f32[48,128]{1,0:T(8,128)S(1)}, f32[48,128]{1,0:T(8,128)}, u32[]{:S(2)}, u32[]{:S(2)}) collective-permute-start(f32[48,128]{1,0:T(8,128)S(1)} %get-tuple-element.683), channel_id=1, source_target_pairs={{0,4},{4,8},{8,12},{12,16},{16,20},{20,24},{24,28},{1,5},{5,9},{9,... | collective-permute-start | bytes 73736
  613.2 10.8 collective-permute-start.2
  627.3 42.8 %copy-start.98 = (f32[1,1,2048]{2,1,0:T(1,128)S(1)}, f32[1,1,2048]{2,1,0:T(1,128)}, u32[]{:S(2)}) copy-start(f32[1,1,2048]{2,1,0:T(1,128)} %copy-done.97) | copy-start | bytes 24580
  627.3 42.8 %copy-start.112 = (f32[1,1,2048]{2,1,0:T(1,128)S(1)}, f32[1,1,2048]{2,1,0:T(1,128)}, u32[]{:S(2)}) copy-start(f32[1,1,2048]{2,1,0:T(1,128)} %copy-done.111) | copy-start | bytes 24580
  670.1 9.7 copy-start.115
  713.0 61.0 %copy-start.134 = (f32[2048]{0:T(1024)S(1)}, f32[2048]{0:T(1024)}, u32[]{:S(2)}) copy-start(f32[2048]{0:T(1024)} %get-tuple-element.797) | copy-start | bytes 24580
  774.0 19.5 %copy-start.105 = (f32[1,1,2048]{2,1,0:T(1,128)}, f32[1,1,2048]{2,1,0:T(1,128)S(1)}, u32[]{:S(2)}) copy-start(f32[1,1,2048]{2,1,0:T(1,128)S(1)} %get-tuple-element.780) | copy-start | bytes 24580
  774.1 19.5 %slice-start = ((s8[6619136]{0:T(1024)(128)(4,1)}), s8[4194304]{0:T(1024)(128)(4,1)S(1)}, s32[]{:S(2)}) async-start(s8[6619136]{0:T(1024)(128)(4,1)} %bitcast.462), calls=%async_computation.11 | async-start | bytes 8388608
  774.1 19.5 %slice-start.2 = ((s8[6619136]{0:T(1024)(128)(4,1)}), s8[4194304]{0:T(1024)(128)(4,1)S(1)}, s32[]{:S(2)}) async-start(s8[6619136]{0:T(1024)(128)(4,1)} %bitcast.464), calls=%async_computation.13 | async-start | bytes 8388608
  782.7 10.9 slice-start.1
  782.7 10.9 slice-start.3
  797.2 45.5 %copy-start.161 = (f32[512]{0:T(512)S(1)}, f32[512]{0:T(512)}, u32[]{:S(2)}) copy-start(f32[512]{0:T(512)} %get-tuple-element.829) | copy-start | bytes 6148
  842.7 54.6 %copy-start.147 = (f32[1,1,512]{2,1,0:T(1,128)}, f32[1,1,512]{2,1,0:T(1,128)S(1)}, u32[]{:S(2)}) copy-start(f32[1,1,512]{2,1,0:T(1,128)S(1)} %get-tuple-element.802) | copy-start | bytes 6148
  858.9 9.1 copy-start.27
  858.9 9.1 copy-start.63
  858.9 9.1 copy-start.132
  869.3 290.3 %reduce-scatter.20.cloned.1.call-start = ((), (), s32[]{:S(2)}) async-start(), calls=%async_computation.7 | async-start | bytes 4718592 | tf_op jit(solution)/shard_map/reduce_scatter | solution.py:373
  883.2 14.1 copy-start.57
  883.2 14.1 copy-start.160
  942.3 263.7 %reduce-scatter.16.cloned.1.call-start = ((), (), s32[]{:S(2)}) async-start(), calls=%async_computation.5 | async-start | bytes 4718592 | tf_op jit(solution)/shard_map/reduce_scatter | solution.py:371
  1059.7 46.9 %copy-start.159 = (f32[512]{0:T(512)S(1)}, f32[512]{0:T(512)}, u32[]{:S(2)}) copy-start(f32[512]{0:T(512)} %get-tuple-element.827) | copy-start | bytes 6148
  1118.4 255.2 %reduce-scatter.18.cloned.1.call-start = ((), (), s32[]{:S(2)}) async-start(), calls=%async_computation.6 | async-start | bytes 10616832 | tf_op jit(solution)/shard_map/reduce_scatter | solution.py:372
  1136.9 522.7 %reduce-scatter.22.cloned.1.call-start = ((), (), s32[]{:S(2)}) async-start(), calls=%async_computation.8 | async-start | bytes 18874368 | tf_op jit(solution)/shard_map/reduce_scatter | solution.py:374
  1148.7 568.0 %all-reduce.68.cloned.1.call-start = ((), (), s32[]{:S(2)}) async-start(), calls=%async_computation.10 | async-start | bytes 4456448 | tf_op jit(solution)/shard_map/psum | solution.py:378
  1681.7 12.9 copy-start.10
  (135 other events, 475.5 us)
Sparse Core Ops, SparseCore 0:
  869.4 64.0 reduce-scatter.23
  942.4 88.4 reduce-scatter.19
  1118.5 87.3 reduce-scatter.15
  1210.4 163.1 reduce-scatter.17
  1377.8 281.8 reduce-scatter.21
  1663.4 53.3 all-reduce.67
where the time goes:
time: 1750 us; the launch traced here: 1730 us
  waiting for transfers between devices  514 us (29%)
  local copies, waits for them, and re-layouts  446 us (25%)
  blocking collectives  443 us (25%)
  matrix products  167 us (10%)
  other arithmetic  128 us (7%)
  between operations  19.1 us (1%)
    reduce_scatter x1, waiting for transfers between devices, body(): lax.psum_scatter(weight_accum[3], 'dp', scatter_dimension=0, tiled=True)  284 us
    reduce_scatter x1, waiting for transfers between devices, body(): lax.psum_scatter(weight_accum[1], 'dp', scatter_dimension=0, tiled=True)  166 us
    psum x4, blocking collectives, forward_norm(): totals = lax.psum(stacked, ('dp', 'narrow'))  163 us
    psum x4, blocking collectives, backward_norm(): totals = lax.psum(stacked, ('dp', 'narrow'))  161 us
    unnamed x453, local copies, waits for them, and re-layouts  104 us
    slice x22, local copies, waits for them, and re-layouts, gather_taps(): tap_grid[:, :, :, 3 * tap_row + tap_col, :]  94.5 us
    all_gather x2, blocking collectives, body(): candidates = lax.all_gather(unit_low, 'dp', axis=1, tiled=True)  63 us
    concatenate x36, local copies, waits for them, and re-layouts, spread_taps(): return jnp.concatenate(pieces, axis=-1).reshape(-1, 9 * hidden.shape[-1])  62.7 us
  transfers between devices with their start and end apart: 12, of which 4 were waited for; matrix products, arithmetic and copies ran while one was open for 18% of the time, Pallas kernels for 0%

commit v1 on v0

v1 whole, which is shorter than its diff:
```python
import functools
import math

import jax
import jax.numpy as jnp
import numpy as np
from jax import lax
from jax.experimental import pallas as pl
from jax.experimental.pallas import tpu as pltpu
from jax.sharding import PartitionSpec as P

VIEWS = 2
CROPS = 4
VSIDE = 7
CSIDE = 3
TAU_INV = 10.0
EPS = 1e-05
LEN_EPS = 1e-06
BOTH = ("dp", "narrow")
F32 = jnp.float32
BF16 = jnp.bfloat16
MIB = 1 << 20


def round_up(value, step):
    return -(-value // step) * step


def xor_permute(array, offset, count):
    return lax.ppermute(array, BOTH, [(i, i ^ offset) for i in range(count)])


def bit_stages(first, last):
    bits = [1 << b for b in range(first, last)]
    stages = [bits[:1]] if bits else []
    rest = bits[1:]
    while rest:
        stages.append(rest[:2])
        rest = rest[2:]
    return stages


def all_sum(array, count):
    for stage in bit_stages(0, count.bit_length() - 1):
        if len(stage) == 1:
            array = array + xor_permute(array, stage[0], count)
        else:
            low, high = stage
            near = xor_permute(array, low, count)
            far = xor_permute(array, high, count)
            across = xor_permute(array, low ^ high, count)
            array = (array + near) + (far + across)
    return array


def gather_all(array, count):
    parts = [array]
    stages = bit_stages(0, count.bit_length() - 1)
    for stage in stages[:0:-1] + stages[:1]:
        offsets = stage if len(stage) == 1 else [stage[0], stage[1], stage[0] ^ stage[1]]
        block = jnp.stack(parts) if len(parts) > 1 else parts[0][None]
        arrived = [xor_permute(block, off, count) for off in offsets]
        parts = [p for p in parts]
        for got in arrived:
            parts.extend(got[k] for k in range(got.shape[0]))
    return jnp.stack(parts)


def gather_order(count):
    order = [0]
    stages = bit_stages(0, count.bit_length() - 1)
    for stage in stages[:0:-1] + stages[:1]:
        offsets = stage if len(stage) == 1 else [stage[0], stage[1], stage[0] ^ stage[1]]
        order = order + [o ^ off for off in offsets for o in order]
    return np.array(order, np.int32)


def dot(left, right):
    return jnp.dot(left, right, preferred_element_type=F32)


def dot_nt(left, right):
    return lax.dot_general(left, right, (((1,), (1,)), ((), ())), preferred_element_type=F32)


def sigmoid(values):
    return 0.5 * jnp.tanh(0.5 * values) + 0.5


def silu_slope(values):
    sigma = sigmoid(values)
    return sigma * (1.0 + values * (1.0 - sigma))


def norm_terms(totals, rows):
    means = totals[0:1] / rows
    variance = totals[1:2] / rows - means * means
    return means, lax.rsqrt(variance + EPS)


def halves(values):
    high = values.astype(BF16)
    return high, (values - high.astype(F32)).astype(BF16)


def col_sums(first, second):
    return jnp.sum(first, axis=0, keepdims=True), jnp.sum(second, axis=0, keepdims=True)


class Sizes:
    def __init__(self, view_rows, crop_rows):
        self.views, self.crops = view_rows, crop_rows
        self.crop_at = round_up(view_rows, 16)
        self.rows = self.crop_at + round_up(crop_rows, 16)

    def zero_pads(self, ref, lead, cols):
        zero = jnp.zeros((self.crop_at - self.views, cols), ref.dtype)
        ref[lead, self.views : self.crop_at, :] = zero
        tail = self.rows - self.crop_at - self.crops
        ref[lead, self.crop_at + self.crops :, :] = jnp.zeros((tail, cols), ref.dtype)

    def row_mask(self):
        row = lax.broadcasted_iota(jnp.int32, (self.rows, 128), 0)
        inside = (row < self.views) | ((row >= self.crop_at) & (row < self.crop_at + self.crops))
        return inside


def wide(mask, cols):
    return jnp.concatenate([mask] * (cols // 128), axis=1)


def fill_edges(edges_ref, sizes):
    for start, stop, at, side in (
        (0, sizes.crop_at, sizes.views, VSIDE),
        (sizes.crop_at, sizes.rows, sizes.crop_at + sizes.crops, CSIDE),
    ):
        count = stop - start
        row = lax.broadcasted_iota(jnp.int32, (count, 128), 0)
        real = row < (at - start)
        rowf = row.astype(F32) + 0.5
        line = jnp.floor(rowf * (1.0 / side))
        col = rowf - 0.5 - line * side
        in_map = line - jnp.floor((line + 0.5) * (1.0 / side)) * side
        keep = (col > 0.5, col < side - 1.5, in_map > 0.5, in_map < side - 1.5)
        for k in range(4):
            edges_ref[k, start:stop, :] = jnp.where(real & keep[k], 1.0, 0.0)
        edges_ref[4, start:stop, :] = jnp.where(real, 1.0, 0.0)


PAD = 16


def tap_block(source_ref, edges_ref, sizes, tap, width):
    dy, dx = tap // 3 - 1, tap % 3 - 1
    pieces = []
    for start, stop, side in ((0, sizes.crop_at, VSIDE), (sizes.crop_at, sizes.rows, CSIDE)):
        shift = dy * side + dx
        values = source_ref[PAD + start + shift : PAD + stop + shift, :]
        mask = None
        for cond, plane in ((dx < 0, 0), (dx > 0, 1), (dy < 0, 2), (dy > 0, 3)):
            if cond:
                edge = edges_ref[plane, start:stop, :]
                mask = edge if mask is None else mask * edge
        if mask is None:
            mask = edges_ref[4, start:stop, :]
        pieces.append((values * wide(mask, width)).astype(BF16))
    return jnp.concatenate(pieces, axis=0)


def k_reduce(xv, xc, w, act, stats, *, sizes):
    views = dot(xv[0], w[...])
    crops = dot(xc[0], w[...])
    act[0, : sizes.views, :] = views
    act[0, sizes.crop_at : sizes.crop_at + sizes.crops, :] = crops
    sizes.zero_pads(act, 0, act.shape[2])
    a, b = col_sums(views, views * views)
    c, d = col_sums(crops, crops * crops)
    stats[0, 0:1, :] = a + c
    stats[0, 1:2, :] = b + d


def k_spatial(act, totals, gain, shift, w, hid, act_two, stats, source, edges, *, sizes, rows):
    width = act.shape[2]

    @pl.when(pl.program_id(0) == 0)
    def _():
        fill_edges(edges, sizes)
        source[:PAD, :] = jnp.zeros((PAD, width), F32)
        source[PAD + sizes.rows :, :] = jnp.zeros((PAD, width), F32)

    means, inv = norm_terms(totals[0], rows)
    pre = (act[0] - means) * (inv * gain[...]) + shift[...]
    hidden = (pre * sigmoid(pre)).astype(BF16)
    hid[0] = hidden
    source[PAD : PAD + sizes.rows, :] = hidden.astype(F32)
    for tap in range(9):
        cols = tap_block(source, edges, sizes, tap, width)
        part = dot(cols, w[tap * width : (tap + 1) * width, :])
        if tap == 0:
            act_two[0] = part
        else:
            act_two[0] += part
    out = act_two[0]
    a, b = col_sums(out, out * out)
    stats[0, 0:1, :] = a
    stats[0, 1:2, :] = b


def k_expand(act, totals, gain, shift, w, hid, act_three, stats, *, sizes, rows):
    @pl.when(pl.program_id(1) == 0)
    def _():
        means, inv = norm_terms(totals[0], rows)
        pre = (act[0] - means) * (inv * gain[...]) + shift[...]
        keep = wide(sizes.row_mask(), act.shape[2])
        hid[0] = jnp.where(keep, pre * sigmoid(pre), 0.0).astype(BF16)

    out = dot(hid[0], w[...])
    act_three[0] = out
    a, b = col_sums(out, out * out)
    stats[0, 0:1, :] = a
    stats[0, 1:2, :] = b


def k_pool(act, totals, gain, shift, xv, xc, pool_v, pool_c, inv_count, w, pooled, head, stats, *, sizes, rows, steps):
    step, micro = pl.program_id(0), pl.program_id(1)
    means, inv = norm_terms(totals[0], rows)
    scale = inv * gain[...]

    def block_sum(start, count, x, pool):
        resid = (act[0, start : start + count, :] - means) * scale + shift[...] + x[0].astype(F32)
        high, low = halves(resid * sigmoid(resid))
        return dot(pool[...], high) + dot(pool[...], low)

    total = block_sum(0, sizes.views, xv, pool_v) + block_sum(sizes.crop_at, sizes.crops, xc, pool_c)
    low_pooled = (total * inv_count[...]).astype(BF16)
    pooled[0] = low_pooled
    part = dot(low_pooled, w[...])

    @pl.when(step == 0)
    def _():
        head[micro] = part

    @pl.when(step > 0)
    def _():
        head[micro] += part

    @pl.when(step == steps - 1)
    def _():
        out = head[micro]
        a, b = col_sums(out, out * out)
        stats[micro, 0:1, :] = a
        stats[micro, 1:2, :] = b


def head_forward(head, totals, gain, shift, w_embed, count):
    means, inv = norm_terms(totals, count)
    normed = (head - means) * inv
    pre = normed * gain + shift
    hidden = (pre * sigmoid(pre)).astype(BF16)
    embedding = dot(hidden, w_embed)
    inv_len = lax.rsqrt(jnp.sum(embedding * embedding, axis=1, keepdims=True) + LEN_EPS)
    return normed, pre, inv, hidden, embedding * inv_len, inv_len


def k_embed(head, totals, gain, shift, w_embed, hidden, unit_low, *, count):
    _, _, _, hid, unit, _ = head_forward(head[0], totals[0], gain[...], shift[...], w_embed[...], count)
    hidden[0] = hid
    unit_low[0] = unit.astype(BF16)


def k_loss(
    units, ids_all, ids_own, pos_all, pos_own, head, totals, gain, shift, w_embed,
    loss, slopes, grad_embed, stats, *, count, loss_scale, block,
):
    everyone = units[0]
    n_all = everyone.shape[0]
    n_own = head.shape[1]

    def add_rows(k, sums):
        start = k * block
        rows = units[0, pl.ds(pl.multiple_of(start, block), block), :]
        scores = dot_nt(rows, everyone) * TAU_INV
        mine = lax.broadcasted_iota(jnp.int32, (block, n_all), 0) + start
        other = lax.broadcasted_iota(jnp.int32, (block, n_all), 1)
        terms = jnp.where(mine == other, 0.0, jnp.exp(scores - TAU_INV))
        return sums + jnp.sum(terms, axis=0, keepdims=True)

    sums = lax.fori_loop(0, n_all // block, add_rows, jnp.zeros((1, n_all), F32))
    log_all = jnp.log(sums) + TAU_INV
    normed, pre, inv, hid, unit, inv_len = head_forward(
        head[0], totals[0], gain[...], shift[...], w_embed[...], count
    )
    low = unit.astype(BF16)
    scores = dot_nt(low, everyone) * TAU_INV
    itself = lax.broadcasted_iota(jnp.int32, (n_own, n_all), 0) == lax.broadcasted_iota(
        jnp.int32, (n_own, n_all), 1
    )
    own_sum = jnp.sum(jnp.where(itself, 0.0, jnp.exp(scores - TAU_INV)), axis=1, keepdims=True)
    log_own = jnp.log(own_sum) + TAU_INV
    positive = (ids_own[0] == ids_all[0]) & jnp.logical_not(itself)
    pos_sum = jnp.sum(jnp.where(positive, scores, 0.0), axis=1, keepdims=True)
    loss[0] = log_own - pos_sum * pos_own[0]
    by_row = jnp.where(itself, 0.0, jnp.exp(scores - log_own)) - jnp.where(positive, pos_own[0], 0.0)
    by_col = jnp.where(itself, 0.0, jnp.exp(scores - log_all)) - jnp.where(positive, pos_all[0], 0.0)
    grad_unit = (
        dot((by_row * loss_scale).astype(BF16), everyone)
        + dot((by_col * loss_scale).astype(BF16), everyone)
    ) * TAU_INV
    grad = inv_len * (grad_unit - unit * jnp.sum(unit * grad_unit, axis=1, keepdims=True))
    grad_low = grad.astype(BF16)
    grad_embed[0] = grad_low
    slope = dot_nt(grad_low, w_embed[...]) * silu_slope(pre)
    slopes[0] = slope
    a, b = col_sums(slope, slope * normed)
    stats[0, 0:1, :] = a
    stats[0, 1:2, :] = b


def norm_back(slopes, normed, sums, gain, inv, rows):
    return (gain * inv) * (slopes - sums[0:1] / rows - normed * (sums[1:2] / rows))


def k_back_pool(
    slopes, head, tot_head, sum_head, gain_head, act, totals, gain, shift, xv, xc,
    spread_v, spread_c, inv_count, w, grad_head, grad_resid, stats, held, *, sizes, rows, count,
):
    micro = pl.program_id(1)

    @pl.when(pl.program_id(0) == 0)
    def _():
        means, inv = norm_terms(tot_head[micro], count)
        normed = (head[micro] - means) * inv
        out = norm_back(slopes[micro], normed, sum_head[micro], gain_head[...], inv, count)
        held[micro] = out.astype(BF16)
        grad_head[micro] = out.astype(BF16)

    high, low = halves(dot_nt(held[micro], w[...]) * inv_count[...])
    means, inv = norm_terms(totals[0], rows)
    tot = []
    for start, n, x, spread in (
        (0, sizes.views, xv, spread_v),
        (sizes.crop_at, sizes.crops, xc, spread_c),
    ):
        normed = (act[0, start : start + n, :] - means) * inv
        resid = normed * gain[...] + shift[...] + x[0].astype(F32)
        back = dot(spread[...], high) + dot(spread[...], low)
        slope = back * silu_slope(resid)
        grad_resid[0, start : start + n, :] = slope
        tot.append(col_sums(slope, slope * normed))
    sizes.zero_pads(grad_resid, 0, grad_resid.shape[2])
    stats[0, 0:1, :] = tot[0][0] + tot[1][0]
    stats[0, 1:2, :] = tot[0][1] + tot[1][1]


def k_back_expand(
    grad_resid, act_three, tot_three, sum_three, gain_three, w, act_two, tot_two, gain_two, shift_two,
    grad_three, slopes, stats, acc, *, sizes, rows, steps,
):
    step = pl.program_id(1)
    means, inv = norm_terms(tot_three[0], rows)
    normed = (act_three[0] - means) * inv
    grad = norm_back(grad_resid[0], normed, sum_three[0], gain_three[...], inv, rows)
    low = jnp.where(wide(sizes.row_mask(), grad.shape[1]), grad, 0.0).astype(BF16)
    grad_three[0] = low
    part = dot_nt(low, w[...])

    @pl.when(step == 0)
    def _():
        acc[...] = part

    @pl.when(step > 0)
    def _():
        acc[...] += part

    @pl.when(step == steps - 1)
    def _():
        means, inv = norm_terms(tot_two[0], rows)
        normed = (act_two[0] - means) * inv
        slope = acc[...] * silu_slope(normed * gain_two[...] + shift_two[...])
        slopes[0] = slope
        a, b = col_sums(slope, slope * normed)
        stats[0, 0:1, :] = a
        stats[0, 1:2, :] = b


def k_back_spatial(
    slopes, act_two, tot_two, sum_two, gain_two, w, act_one, tot_one, gain_one, shift_one,
    grad_cols, slopes_one, stats, source, edges, *, sizes, rows,
):
    width = act_two.shape[2]

    @pl.when(pl.program_id(0) == 0)
    def _():
        fill_edges(edges, sizes)
        source[:PAD, :] = jnp.zeros((PAD, width), F32)
        source[PAD + sizes.rows :, :] = jnp.zeros((PAD, width), F32)

    means, inv = norm_terms(tot_two[0], rows)
    normed = (act_two[0] - means) * inv
    source[PAD : PAD + sizes.rows, :] = norm_back(slopes[0], normed, sum_two[0], gain_two[...], inv, rows)
    for tap in range(9):
        cols = tap_block(source, edges, sizes, tap, width)
        other = 8 - tap
        grad_cols[0, :, other * width : (other + 1) * width] = cols
        part = dot_nt(cols, w[other * width : (other + 1) * width, :])
        if tap == 0:
            slopes_one[0] = part
        else:
            slopes_one[0] += part
    means, inv = norm_terms(tot_one[0], rows)
    normed = (act_one[0] - means) * inv
    slope = slopes_one[0] * silu_slope(normed * gain_one[...] + shift_one[...])
    slopes_one[0] = slope
    a, b = col_sums(slope, slope * normed)
    stats[0, 0:1, :] = a
    stats[0, 1:2, :] = b


def k_back_reduce(
    slopes, act_one, tot_one, sum_one, gain_one, w, grad_resid, grad_one, grad_v, grad_c, *, sizes, rows
):
    @pl.when(pl.program_id(1) == 0)
    def _():
        means, inv = norm_terms(tot_one[0], rows)
        normed = (act_one[0] - means) * inv
        grad = norm_back(slopes[0], normed, sum_one[0], gain_one[...], inv, rows)
        grad_one[0] = jnp.where(wide(sizes.row_mask(), grad.shape[1]), grad, 0.0).astype(BF16)

    back = dot_nt(grad_one[0], w[...])
    grad_v[0] = grad_resid[0, : sizes.views, :] + back[: sizes.views]
    at = sizes.crop_at
    grad_c[0] = grad_resid[0, at : at + sizes.crops, :] + back[at : at + sizes.crops]


def call(kernel, name, grid, ins, outs, scratch=(), flops=0, vmem=56):
    spec = lambda block, index: pl.BlockSpec(block, index)
    moved = sum(a.size * a.dtype.itemsize for a, _, _ in ins) + sum(
        math.prod(s) * jnp.dtype(t).itemsize for s, t, _, _ in outs
    )
    return pl.pallas_call(
        kernel,
        grid=grid,
        in_specs=[spec(b, i) for _, b, i in ins],
        out_specs=[spec(b, i) for _, _, b, i in outs],
        out_shape=[jax.ShapeDtypeStruct(s, t) for s, t, _, _ in outs],
        scratch_shapes=list(scratch),
        compiler_params=pltpu.CompilerParams(vmem_limit_bytes=vmem * MIB),
        cost_estimate=pl.CostEstimate(flops=int(flops), bytes_accessed=int(moved), transcendentals=0),
        name=name,
    )(*[a for a, _, _ in ins])


def exact(array):
    return lax.optimization_barrier(array)


def add_low(*parts):
    total = parts[0].astype(F32)
    for part in parts[1:]:
        total = total + part.astype(F32)
    return total.astype(BF16)


def reduce_weight(grad, count, data_size, narrow_size):
    rows, cols = grad.shape
    me = lax.axis_index("dp")
    core = lax.axis_index("narrow") % 2
    blocks = grad.reshape(data_size, rows // data_size, cols)
    blocks = jnp.stack(
        [lax.dynamic_index_in_dim(blocks, me ^ j, axis=0, keepdims=False) for j in range(data_size)]
    )
    half = cols // 2
    low, high = blocks[:, :, :half], blocks[:, :, half:]
    keep = jnp.where(core == 0, low, high)
    send = jnp.where(core == 0, high, low)
    part = add_low(keep, xor_permute(send, 1, count))
    size = data_size
    for stage in bit_stages(0, data_size.bit_length() - 1):
        if len(stage) == 1:
            split = part.reshape((size // 2, 2) + part.shape[1:])
            part = add_low(split[:, 0], xor_permute(split[:, 1], stage[0] * narrow_size, count))
            size //= 2
        else:
            split = part.reshape((size // 4, 4) + part.shape[1:])
            got = [
                xor_permute(split[:, k], off * narrow_size, count)
                for k, off in ((1, stage[0]), (2, stage[1]), (3, stage[0] ^ stage[1]))
            ]
            part = add_low(split[:, 0], *got)
            size //= 4
    part = exact(part[0])
    off = 2
    while off < narrow_size:
        part = exact(add_low(part, xor_permute(part, off, count)))
        off *= 2
    other = xor_permute(part, 1, count)
    both = jnp.where(
        core == 0, jnp.concatenate([part, other], axis=1), jnp.concatenate([other, part], axis=1)
    )
    return both.astype(F32)


def body(
    view_maps, crop_maps, image_ids, w_reduce, gain_one, shift_one, w_spatial, gain_two, shift_two,
    w_expand, gain_three, shift_three, w_hidden, gain_head, shift_head, w_embed,
):
    micros, view_rows, channels = view_maps.shape
    crop_rows = crop_maps.shape[1]
    mid = w_reduce.shape[1]
    hidden_width = w_hidden.shape[1]
    emb_width = w_embed.shape[1]
    images_dev = view_rows // (VIEWS * VSIDE * VSIDE)
    each = VIEWS + CROPS
    own = images_dev * each
    data_size, narrow_size = lax.axis_size("dp"), lax.axis_size("narrow")
    count = data_size * narrow_size
    emb_total = own * count
    pixel_count = (view_rows + crop_rows) * count
    loss_scale = 1.0 / (micros * emb_total)
    device = lax.axis_index("dp") * narrow_size + lax.axis_index("narrow")
    sizes = Sizes(view_rows, crop_rows)
    rows = sizes.rows

    pool_v = np.zeros((own, view_rows), np.float32)
    pool_c = np.zeros((own, crop_rows), np.float32)
    area_v, area_c = VSIDE * VSIDE, CSIDE * CSIDE
    for r in range(view_rows):
        image, view = divmod(r // area_v, VIEWS)
        pool_v[image * each + view, r] = 1
    for r in range(crop_rows):
        image, crop = divmod(r // area_c, CROPS)
        pool_c[image * each + VIEWS + crop, r] = 1
    inv_count = np.where(np.arange(own) % each < VIEWS, 1.0 / area_v, 1.0 / area_c)
    inv_count = jnp.asarray(inv_count[:, None], F32)
    spread_v, spread_c = jnp.asarray(pool_v.T, BF16), jnp.asarray(pool_c.T, BF16)
    pool_v, pool_c = jnp.asarray(pool_v, BF16), jnp.asarray(pool_c, BF16)

    place = jnp.asarray(gather_order(count)) ^ device
    same = jnp.sum((image_ids[:, :, None] == image_ids[:, None, :]).astype(F32), axis=2)
    inv_pos = 1.0 / (same * each - 1.0)

    from_device = place[:, None] == jnp.arange(count, dtype=jnp.int32)[None, :]

    def by_place(values):
        blocks = values.reshape(micros, 1, count, images_dev)
        moved = jnp.sum(jnp.where(from_device[None, :, :, None], blocks, 0), axis=2)
        return jnp.repeat(moved.reshape(micros, -1), each, axis=1)

    ids_all, pos_all = by_place(image_ids), by_place(inv_pos)
    ids_own, pos_own = ids_all[:, :own, None], pos_all[:, :own, None]
    ids_all, pos_all = ids_all[:, None, :], pos_all[:, None, :]

    row = lambda v: v.reshape(1, -1)
    g1, b1, g2, b2 = row(gain_one), row(shift_one), row(gain_two), row(shift_two)
    g3, b3, gh, bh = row(gain_three), row(shift_three), row(gain_head), row(shift_head)
    reduce_all = lambda stats: all_sum(stats, count)
    flops = 2.0 * micros * rows * channels * mid

    m0 = lambda m: (m, 0, 0)
    fix2 = lambda *_: (0, 0)
    fix3 = lambda *_: (0, 0, 0)
    act_one, st = call(
        functools.partial(k_reduce, sizes=sizes), "reduce", (micros,),
        [
            (view_maps, (1, view_rows, channels), m0),
            (crop_maps, (1, crop_rows, channels), m0),
            (w_reduce, (channels, mid), fix2),
        ],
        [
            ((micros, rows, mid), F32, (1, rows, mid), m0),
            ((micros, 2, mid), F32, (1, 2, mid), m0),
        ],
        flops=flops,
    )
    tot_one = reduce_all(st)
    hid_one, act_two, st = call(
        functools.partial(k_spatial, sizes=sizes, rows=pixel_count), "spatial", (micros,),
        [
            (act_one, (1, rows, mid), m0),
            (tot_one, (1, 2, mid), m0),
            (g1, (1, mid), fix2),
            (b1, (1, mid), fix2),
            (w_spatial, (9 * mid, mid), fix2),
        ],
        [
            ((micros, rows, mid), BF16, (1, rows, mid), m0),
            ((micros, rows, mid), F32, (1, rows, mid), m0),
            ((micros, 2, mid), F32, (1, 2, mid), m0),
        ],
        scratch=[pltpu.VMEM((rows + 2 * PAD, mid), F32), pltpu.VMEM((5, rows, 128), F32)],
        flops=flops * 9 * mid / channels,
    )
    tot_two = reduce_all(st)
    mn0 = lambda m, n: (m, 0, 0)
    mn = lambda m, n: (m, 0, n)
    blk = 512
    steps = channels // blk
    hid_two, act_three, st = call(
        functools.partial(k_expand, sizes=sizes, rows=pixel_count), "expand", (micros, steps),
        [
            (act_two, (1, rows, mid), mn0),
            (tot_two, (1, 2, mid), mn0),
            (g2, (1, mid), fix2),
            (b2, (1, mid), fix2),
            (w_expand, (mid, blk), lambda m, n: (0, n)),
        ],
        [
            ((micros, rows, mid), BF16, (1, rows, mid), mn0),
            ((micros, rows, channels), F32, (1, rows, blk), mn),
            ((micros, 2, channels), F32, (1, 2, blk), mn),
        ],
        flops=flops,
    )
    tot_three = reduce_all(st)
    cblk = 256
    csteps = channels // cblk
    nm = lambda n, m: (m, 0, n)
    vec = lambda n, m: (0, n)
    wrow = lambda n, m: (n, 0)
    pooled, head, st = call(
        functools.partial(k_pool, sizes=sizes, rows=pixel_count, steps=csteps), "pool", (csteps, micros),
        [
            (act_three, (1, rows, cblk), nm),
            (tot_three, (1, 2, cblk), nm),
            (g3, (1, cblk), vec),
            (b3, (1, cblk), vec),
            (view_maps, (1, view_rows, cblk), nm),
            (crop_maps, (1, crop_rows, cblk), nm),
            (pool_v, (own, view_rows), fix2),
            (pool_c, (own, crop_rows), fix2),
            (inv_count, (own, 1), fix2),
            (w_hidden, (cblk, hidden_width), wrow),
        ],
        [
            ((micros, own, channels), BF16, (1, own, cblk), nm),
            ((micros, own, hidden_width), F32, (micros, own, hidden_width), fix3),
            ((micros, 2, hidden_width), F32, (micros, 2, hidden_width), fix3),
        ],
        flops=flops / 10,
    )
    tot_head = reduce_all(st)
    head_in = [
        (head, (1, own, hidden_width), m0),
        (tot_head, (1, 2, hidden_width), m0),
        (gh, (1, hidden_width), fix2),
        (bh, (1, hidden_width), fix2),
        (w_embed, (hidden_width, emb_width), fix2),
    ]
    head_hid, unit_low = call(
        functools.partial(k_embed, count=emb_total), "embed", (micros,), head_in,
        [
            ((micros, own, hidden_width), BF16, (1, own, hidden_width), m0),
            ((micros, own, emb_width), BF16, (1, own, emb_width), m0),
        ],
    )
    units = gather_all(unit_low, count)
    units = jnp.transpose(units, (1, 0, 2, 3)).reshape(micros, emb_total, emb_width)
    loss, slopes, grad_embed, st = call(
        functools.partial(k_loss, count=emb_total, loss_scale=loss_scale, block=128), "loss", (micros,),
        [
            (units, (1, emb_total, emb_width), m0),
            (ids_all, (1, 1, emb_total), m0),
            (ids_own, (1, own, 1), m0),
            (pos_all, (1, 1, emb_total), m0),
            (pos_own, (1, own, 1), m0),
        ]
        + head_in,
        [
            ((micros, own, 1), F32, (1, own, 1), m0),
            ((micros, own, hidden_width), F32, (1, own, hidden_width), m0),
            ((micros, own, emb_width), BF16, (1, own, emb_width), m0),
            ((micros, 2, hidden_width), F32, (1, 2, hidden_width), m0),
        ],
    )
    sum_head = reduce_all(st)

    grad_head, grad_resid, st = call(
        functools.partial(k_back_pool, sizes=sizes, rows=pixel_count, count=emb_total), "back_pool",
        (csteps, micros),
        [
            (slopes, (micros, own, hidden_width), fix3),
            (head, (micros, own, hidden_width), fix3),
            (tot_head, (micros, 2, hidden_width), fix3),
            (sum_head, (micros, 2, hidden_width), fix3),
            (gh, (1, hidden_width), fix2),
            (act_three, (1, rows, cblk), nm),
            (tot_three, (1, 2, cblk), nm),
            (g3, (1, cblk), vec),
            (b3, (1, cblk), vec),
            (view_maps, (1, view_rows, cblk), nm),
            (crop_maps, (1, crop_rows, cblk), nm),
            (spread_v, (view_rows, own), fix2),
            (spread_c, (crop_rows, own), fix2),
            (inv_count, (own, 1), fix2),
            (w_hidden, (cblk, hidden_width), wrow),
        ],
        [
            ((micros, own, hidden_width), BF16, (micros, own, hidden_width), fix3),
            ((micros, rows, channels), F32, (1, rows, cblk), nm),
            ((micros, 2, channels), F32, (1, 2, cblk), nm),
        ],
        scratch=[pltpu.VMEM((micros, own, hidden_width), BF16)],
        flops=flops / 10,
    )
    sum_three = reduce_all(st)
    grad_three, slopes_two, st = call(
        functools.partial(k_back_expand, sizes=sizes, rows=pixel_count, steps=steps), "back_expand",
        (micros, steps),
        [
            (grad_resid, (1, rows, blk), mn),
            (act_three, (1, rows, blk), mn),
            (tot_three, (1, 2, blk), mn),
            (sum_three, (1, 2, blk), mn),
            (g3, (1, blk), lambda m, n: (0, n)),
            (w_expand, (mid, blk), lambda m, n: (0, n)),
            (act_two, (1, rows, mid), mn0),
            (tot_two, (1, 2, mid), mn0),
            (g2, (1, mid), fix2),
            (b2, (1, mid), fix2),
        ],
        [
            ((micros, rows, channels), BF16, (1, rows, blk), mn),
            ((micros, rows, mid), F32, (1, rows, mid), mn0),
            ((micros, 2, mid), F32, (1, 2, mid), mn0),
        ],
        scratch=[pltpu.VMEM((rows, mid), F32)],
        flops=flops,
    )
    sum_two = reduce_all(st)
    grad_cols, slopes_one, st = call(
        functools.partial(k_back_spatial, sizes=sizes, rows=pixel_count), "back_spatial", (micros,),
        [
            (slopes_two, (1, rows, mid), m0),
            (act_two, (1, rows, mid), m0),
            (tot_two, (1, 2, mid), m0),
            (sum_two, (1, 2, mid), m0),
            (g2, (1, mid), fix2),
            (w_spatial, (9 * mid, mid), fix2),
            (act_one, (1, rows, mid), m0),
            (tot_one, (1, 2, mid), m0),
            (g1, (1, mid), fix2),
            (b1, (1, mid), fix2),
        ],
        [
            ((micros, rows, 9 * mid), BF16, (1, rows, 9 * mid), m0),
            ((micros, rows, mid), F32, (1, rows, mid), m0),
            ((micros, 2, mid), F32, (1, 2, mid), m0),
        ],
        scratch=[pltpu.VMEM((rows + 2 * PAD, mid), F32), pltpu.VMEM((5, rows, 128), F32)],
        flops=flops * 9 * mid / channels,
    )
    sum_one = reduce_all(st)
    grad_one, grad_views, grad_crops = call(
        functools.partial(k_back_reduce, sizes=sizes, rows=pixel_count), "back_reduce", (micros, steps),
        [
            (slopes_one, (1, rows, mid), mn0),
            (act_one, (1, rows, mid), mn0),
            (tot_one, (1, 2, mid), mn0),
            (sum_one, (1, 2, mid), mn0),
            (g1, (1, mid), fix2),
            (w_reduce, (blk, mid), lambda m, n: (n, 0)),
            (grad_resid, (1, rows, blk), mn),
        ],
        [
            ((micros, rows, mid), BF16, (1, rows, mid), mn0),
            (view_maps.shape, F32, (1, view_rows, blk), mn),
            (crop_maps.shape, F32, (1, crop_rows, blk), mn),
        ],
        flops=flops,
    )

    over = lambda a, b: jnp.einsum("mri,mrj->ij", a, b, preferred_element_type=F32)
    reduce_w = lambda g: reduce_weight(g.astype(BF16), count, data_size, narrow_size)
    gw_embed = reduce_w(over(head_hid, grad_embed))
    gw_hidden = reduce_w(over(pooled, grad_head))
    gw_expand = reduce_w(over(hid_two, grad_three))
    by_tap = jnp.einsum(
        "mri,mrtj->tij", hid_one, grad_cols.reshape(micros, rows, 9, mid), preferred_element_type=F32
    )
    gw_spatial = reduce_w(by_tap.reshape(9 * mid, mid))
    at = sizes.crop_at
    gw_reduce = reduce_w(
        over(view_maps, grad_one[:, :view_rows]) + over(crop_maps, grad_one[:, at : at + crop_rows])
    )
    gain_grad = lambda sums: jnp.sum(sums[:, 1], axis=0)
    shift_grad = lambda sums: jnp.sum(sums[:, 0], axis=0)
    return (
        loss.reshape(micros, own), grad_views, grad_crops,
        gw_reduce, gain_grad(sum_one), shift_grad(sum_one),
        gw_spatial, gain_grad(sum_two), shift_grad(sum_two),
        gw_expand, gain_grad(sum_three), shift_grad(sum_three),
        gw_hidden, gain_grad(sum_head), shift_grad(sum_head),
        gw_embed,
    )


def solution(mesh):
    rows = P(None, BOTH, None)
    return jax.shard_map(
        body,
        mesh=mesh,
        in_specs=(rows, rows) + (P(),) * 14,
        out_specs=(
            P(None, BOTH), rows, rows,
            P("dp", None), P(), P(),
            P("dp", None), P(), P(),
            P("dp", None), P(), P(),
            P("dp", None), P(), P(),
            P("dp", None),
        ),
        check_vma=False,
    )
```

time: 1750 us -> 579 us (0.33)
  blocking collectives: 443 us -> 0 us
  local copies, waits for them, and re-layouts: 446 us -> 70.9 us
  waiting for transfers between devices: 514 us -> 175 us
  Pallas kernels: 0 us -> 155 us
  matrix products: 167 us -> 32.1 us
  other arithmetic: 128 us -> 38.8 us
  starting transfers between devices: 15 us -> 100 us
    reduce_scatter x5 -> x0, waiting for transfers between devices: 494 us -> none  [the longest x1 284 us: body(): lax.psum_scatter(weight_accum[3], 'dp', scatter_dimension=0, tiled=True)]
    psum x8 -> x0, blocking collectives: 324 us -> none  [the longest x4 163 us: forward_norm(): totals = lax.psum(stacked, ('dp', 'narrow'))]
    ppermute x0 -> x98, waiting for transfers between devices: none -> 175 us  [xor_permute(): return lax.ppermute(array, BOTH, [(i, i ^ offset) for i in range(count)])]
    slice x53 -> x0, local copies, waits for them, and re-layouts: 169 us -> none  [the longest x22 94.5 us: gather_taps(): tap_grid[:, :, :, 3 * tap_row + tap_col, :]]
    pallas_call x0 -> x10, Pallas kernels: none -> 155 us  [call(): pl.pallas_call(kernel, grid=grid, in_specs=[spec(b, i) for _, b, i in ins...]
    dot_general x36 -> x6, matrix products: 167 us -> 32.1 us  [the longest x5 19.5 us: body(): jnp.einsum('mri,mrj->ij', a, b, preferred_element_type=F32)]
    ppermute x0 -> x98, starting transfers between devices: none -> 100 us  [xor_permute(): return lax.ppermute(array, BOTH, [(i, i ^ offset) for i in range(count)])]
    all_gather x4 -> x0, blocking collectives: 74.7 us -> none  [the longest x2 63 us: body(): candidates = lax.all_gather(unit_low, 'dp', axis=1, tiled=True)]
  transfers between devices with their start and end apart: 12 -> 98, of which waited for: 4 -> 64; matrix products, arithmetic and copies ran while one was open for 18% -> 22% of each run, Pallas kernels for 0% -> 15%
where the time goes in v1:
time: 579 us; the launch traced here: 574 us
  waiting for transfers between devices  175 us (30%)
  Pallas kernels  155 us (27%)
  starting transfers between devices  100 us (17%)
  local copies, waits for them, and re-layouts  70.9 us (12%)
  other arithmetic  38.8 us (7%)
  matrix products  32.1 us (6%)
    ppermute x98, waiting for transfers between devices, xor_permute(): return lax.ppermute(array, BOTH, [(i, i ^ offset) for i in range(count)])  175 us
    pallas_call x10, Pallas kernels, call(): pl.pallas_call(kernel, grid=grid, in_specs=[spec(b, i) for _, b, i in ins...  155 us
    ppermute x98, starting transfers between devices, xor_permute(): return lax.ppermute(array, BOTH, [(i, i ^ offset) for i in range(count)])  100 us
    unnamed x98, local copies, waits for them, and re-layouts  40.6 us
    pallas_call x1, local copies, waits for them, and re-layouts, call(): pl.pallas_call(kernel, grid=grid, in_specs=[spec(b, i) for _, b, i in ins...  20.1 us
    dot_general x5, matrix products, body(): jnp.einsum('mri,mrj->ij', a, b, preferred_element_type=F32)  19.5 us
    convert_element_type x10, other arithmetic, add_low(): return total.astype(BF16)  12.8 us
    dot_general x1, matrix products, body(): jnp.einsum('mri,mrtj->tij', hid_one, grad_cols.reshape(micros, rows, 9, m...  12.6 us
  transfers between devices with their start and end apart: 98, of which 64 were waited for; matrix products, arithmetic and copies ran while one was open for 22% of the time, Pallas kernels for 15%

profile of v1, /device:TPU:0, one launch (start us, length us, event | category | flops | bytes accessed | tf_op | source)
XLA Modules:
  0.0 574.1 jit_solution(7433408921587246465)
XLA Ops:
  0.6 6.8 %copy.82.xv = bf16[2,588,2048]{2,1,0:T(8,128)(2,1)} copy(bf16[2,588,2048]{2,0,1:T(2,128)(2,1)} %param.22) | data formatting | bytes 9633792 | tf_op args[0]
  7.4 7.8 %reduce.10 = (f32[2,816,512]{2,1,0:T(8,128)}, f32[2,2,512]{2,1,0:T(2,128)}) custom-call(bf16[2,588,2048]{2,1,0:T(8,128)(2,1)} %copy.82.xv, bf16[2,216,2048]{2,1,0:T(8,128)(2,1)} %xc.5, bf16[2048,512]{1,0:T(8,128)(2,1)} %w.15), custom_call_target="tpu_custom_call" | custom-call | flops 3422552064 | bytes 12034048 | tf_op jit(solution)/shard_map/reduce/pallas_call | solution.py:440
  17.4 3.8 collective-permute-start.3
  22.8 2.0 collective-permute-done.2
  25.4 3.7 collective-permute-start.6
  30.9 2.7 collective-permute-done.5
  34.2 13.2 %spatial.1 = (bf16[2,816,512]{2,1,0:T(8,128)(2,1)}, f32[2,816,512]{2,1,0:T(8,128)}, f32[2,2,512]{2,1,0:T(2,128)}) custom-call(f32[2,816,512]{2,1,0:T(8,128)} %get-tuple-element.45.act.act_one, f32[2,2,512]{2,1,0:T(2,128)} %add_add_fusion.14.totals.tot_one, f32[1,512]{1,0:T(1,128)} %bitcast.254, f32[1,512]{1,0:T(1,128)} %bitcast.257, bf16[4608,512]{1,0:T(8,128)(2,1)} %w.14), custom_call_target="tpu_custom_call" | custom-call | flops 7700742144 | bytes 13094912 | tf_op jit(solution)/shard_map/spatial/pallas_call | solution.py:440
  55.1 1.6 collective-permute-start.13
  57.3 2.3 collective-permute-start.11
  61.9 13.2 %expand.1 = (bf16[2,816,512]{2,1,0:T(8,128)(2,1)}, f32[2,816,2048]{2,1,0:T(8,128)}, f32[2,2,2048]{2,1,0:T(2,128)}) custom-call(f32[2,816,512]{2,1,0:T(8,128)} %get-tuple-element.47.act.act_two, f32[2,2,512]{2,1,0:T(2,128)} %add_add_fusion.12.totals.tot_two, f32[1,512]{1,0:T(1,128)} %bitcast.251, f32[1,512]{1,0:T(1,128)} %bitcast.249, bf16[512,2048]{1,0:T(8,128)(2,1)} %w.13), custom_call_target="tpu_custom_call" | custom-call | flops 3422552064 | bytes 20525056 | tf_op jit(solution)/shard_map/expand/pallas_call | solution.py:440
  77.3 2.5 collective-permute-start.17
  84.3 2.6 collective-permute-start.20
  92.7 23.1 %pool.1 = (bf16[2,36,2048]{2,1,0:T(8,128)(2,1)}, f32[2,36,2048]{2,1,0:T(8,128)}, f32[2,2,2048]{2,1,0:T(2,128)}) custom-call(f32[2,816,2048]{2,1,0:T(8,128)} %get-tuple-element.49.act.act_three, f32[2,2,2048]{2,1,0:T(2,128)} %add_add_fusion.6.totals.tot_three, f32[1,2048]{1,0:T(1,128)} %bitcast.242, f32[1,2048]{1,0:T(1,128)} %bitcast.247, ...), custom_call_target="tpu_custom_call" | custom-call | flops 342255200 | bytes 29369008 | tf_op jit(solution)/shard_map/pool/pallas_call | solution.py:440
  126.2 2.3 collective-permute-start.25
  131.2 2.7 embed.1
  134.0 2.5 collective-permute-start.30
  139.8 1.6 collective-permute-done.29
  142.3 2.5 collective-permute-start.33
  145.9 3.9 collective-permute-done.31
  154.2 10.7 %loss.1 = (f32[2,36,1]{2,1,0:T(8,128)}, f32[2,36,2048]{2,1,0:T(8,128)}, bf16[2,36,128]{2,1,0:T(8,128)(2,1)}, f32[2,2,2048]{2,1,0:T(2,128)}) custom-call(bf16[2,1152,128]{2,1,0:T(8,128)(2,1)} %copy.89.units, s32[2,1,1152]{2,1,0:T(1,128)} %broadcast_in_dim_reshape.8.ids_all, s32[2,36,1]{2,1,0:T(8,128)} %copy.91.ids_own, ...), custom_call_target="tpu_custom_call" | custom-call | bytes 2413408 | tf_op jit(solution)/shard_map/loss/pallas_call | solution.py:440
  176.1 2.0 collective-permute-start.39
  181.0 28.9 %back_pool.1 = (bf16[2,36,2048]{2,1,0:T(8,128)(2,1)}, f32[2,816,2048]{2,1,0:T(8,128)}, f32[2,2,2048]{2,1,0:T(2,128)}) custom-call(f32[2,36,2048]{2,1,0:T(8,128)} %get-tuple-element.55.slopes, f32[2,36,2048]{2,1,0:T(8,128)} %get-tuple-element.51.head, f32[2,2,2048]{2,1,0:T(2,128)} %add_add_fusion.4.totals.tot_head, f32[2,2,2048]{2,1,0:T(2,128)} %add_add_fusion.2.sum_head, ...), custom_call_target="tpu_custom_call" | custom-call | flops 342255200 | bytes 43401904 | tf_op jit(solution)/shard_map/back_pool/pallas_call | solution.py:440
  210.0 3.3 bitcast_convert_fusion
  214.6 2.5 collective-permute-start.45
  218.2 2.2 broadcast_select_fusion
  221.6 2.4 collective-permute-start.48
  229.8 20.7 %back_expand.1 = (bf16[2,816,2048]{2,1,0:T(8,128)(2,1)}, f32[2,816,512]{2,1,0:T(8,128)}, f32[2,2,512]{2,1,0:T(2,128)}) custom-call(f32[2,816,2048]{2,1,0:T(8,128)} %get-tuple-element.57.grad_resid, f32[2,816,2048]{2,1,0:T(8,128)} %get-tuple-element.49.act.act_three, f32[2,2,2048]{2,1,0:T(2,128)} %add_add_fusion.6.totals.tot_three, ...), custom_call_target="tpu_custom_call" | custom-call | flops 3422552064 | bytes 42299392 | tf_op jit(solution)/shard_map/back_expand/pallas_call | solution.py:440
  250.5 7.5 %bitcast_convert_fusion.2 = bf16[512,2048]{1,0:T(8,128)(2,1)S(1)} fusion(bf16[2,816,512]{2,1,0:T(8,128)(2,1)S(1)} %copy-done.17, bf16[2,816,2048]{2,1,0:T(8,128)(2,1)} %get-tuple-element.69), kind=kOutput, calls=%fused_computation.6 | convolution fusion | flops 3423600640 | bytes 10452992 | tf_op jit(solution)/shard_map/mri,mrj->ij/dot_general | solution.py:772
  264.4 1.7 collective-permute-start.55
  266.8 2.0 collective-permute-start.53
  271.3 17.2 %back_spatial.1 = (bf16[2,816,4608]{2,1,0:T(8,128)(2,1)}, f32[2,816,512]{2,1,0:T(8,128)}, f32[2,2,512]{2,1,0:T(2,128)}) custom-call(f32[2,816,512]{2,1,0:T(8,128)} %get-tuple-element.59.slopes, f32[2,816,512]{2,1,0:T(8,128)} %get-tuple-element.47.act.act_two, f32[2,2,512]{2,1,0:T(2,128)} %add_add_fusion.12.totals.tot_two, ...), custom_call_target="tpu_custom_call" | custom-call | flops 7700742144 | bytes 33167360 | tf_op jit(solution)/shard_map/back_spatial/pallas_call | solution.py:440
  288.6 20.1 %copy.105 = bf16[2,816,4608]{1,2,0:T(8,128)(2,1)} copy(bf16[2,816,4608]{2,1,0:T(8,128)(2,1)} %get-tuple-element.66) | data formatting | bytes 30081024 | tf_op jit(solution)/shard_map/back_spatial/pallas_call | solution.py:440
  308.7 12.6 %bitcast_convert_fusion.1 = bf16[9,512,512]{1,2,0:T(8,128)(2,1)S(1)} fusion(bf16[2,816,9,512]{1,3,2,0:T(8,128)(2,1)} %bitcast.199, bf16[2,816,512]{2,1,0:T(8,128)(2,1)S(1)} %copy-done.18), kind=kOutput, calls=%fused_computation.1 | convolution fusion | flops 7703101440 | bytes 21430272 | tf_op jit(solution)/shard_map/mri,mrtj->tij/dot_general | solution.py:777
  322.2 2.4 collective-permute-start.59
  328.8 2.4 collective-permute-start.62
  333.3 1.6 broadcast_select_fusion.1
  336.5 17.4 %back_reduce.1 = (bf16[2,816,512]{2,1,0:T(8,128)(2,1)}, f32[2,588,2048]{2,1,0:T(8,128)}, f32[2,216,2048]{2,1,0:T(8,128)}) custom-call(f32[2,816,512]{2,1,0:T(8,128)} %get-tuple-element.61.slopes, f32[2,816,512]{2,1,0:T(8,128)} %get-tuple-element.45.act.act_one, f32[2,2,512]{2,1,0:T(2,128)} %add_add_fusion.14.totals.tot_one, ...), custom_call_target="tpu_custom_call" | custom-call | flops 3422552064 | bytes 37013504 | tf_op jit(solution)/shard_map/back_reduce/pallas_call | solution.py:440
  354.0 5.2 fusion.7
  359.2 2.3 fusion.2
  361.5 2.7 copy.123
  376.4 2.3 collective-permute-start.95
  380.0 2.2 collective-permute-done.95
  384.8 2.8 collective-permute-done.96
  388.3 21.9 %copy.119 = f32[2,588,2048]{2,0,1:T(2,128)} copy(f32[2,588,2048]{2,1,0:T(8,128)} %get-tuple-element.107) | data formatting | bytes 19267584
  411.0 2.5 add_convert_fusion.2
  416.2 6.8 %add_convert_fusion = bf16[8,256,1024]{2,1,0:T(8,128)(2,1)S(1)} fusion(bf16[8,256,1024]{2,1,0:T(8,128)(2,1)} %collective-permute-done.84, pred[]{:T(512)S(6)} %eq.30, bf16[8,256,2048]{2,1,0:T(8,128)(2,1)} %copy-done), kind=kLoop, calls=%fused_computation.2 | loop fusion | flops 10485760 | bytes 16777216 | tf_op jit(solution)/shard_map/convert_element_type | solution.py:461
  424.3 4.0 collective-permute-done.78
  428.7 1.7 collective-permute-start.81
  430.4 9.1 %collective-permute-done.64 = bf16[4,256,256]{2,1,0:T(8,128)(2,1)S(1)} collective-permute-done((bf16[4,256,256]{2,1,0:T(8,128)(2,1)S(1)}, bf16[4,256,256]{2,1,0:T(8,128)(2,1)S(1)}, u32[]{:S(2)}, u32[]{:S(2)}) %collective-permute-start.64) | collective-permute-done | bytes 524320 | tf_op jit(solution)/shard_map/ppermute | solution.py:30
  440.1 2.7 add_convert_fusion.1
  444.5 1.9 collective-permute-start.65
  446.4 2.2 collective-permute-start.67
  448.7 3.3 collective-permute-done.65
  452.5 2.4 collective-permute-done.67
  454.9 4.2 collective-permute-done.66
  459.8 24.7 %collective-permute-done.85 = bf16[4,256,1024]{2,1,0:T(8,128)(2,1)S(1)} collective-permute-done((bf16[4,256,1024]{2,1,0:T(8,128)(2,1)S(1)}, bf16[4,256,1024]{2,1,0:T(8,128)(2,1)S(1)}, u32[]{:S(2)}, u32[]{:S(2)}) %collective-permute-start.85) | collective-permute-done | bytes 2097184 | tf_op jit(solution)/shard_map/ppermute | solution.py:30
  485.8 1.7 collective-permute-start.88
  487.5 21.8 %collective-permute-done.71 = bf16[4,576,256]{2,1,0:T(8,128)(2,1)S(1)} collective-permute-done((bf16[4,576,256]{2,1,0:T(8,128)(2,1)S(1)}, bf16[4,576,256]{2,1,0:T(8,128)(2,1)S(1)}, u32[]{:S(2)}, u32[]{:S(2)}) %collective-permute-start.71) | collective-permute-done | bytes 1179680 | tf_op jit(solution)/shard_map/ppermute | solution.py:30
  510.2 1.9 collective-permute-start.72
  512.0 2.2 collective-permute-start.74
  514.3 26.7 %collective-permute-done.87 = bf16[1,256,1024]{2,1,0:T(8,128)(2,1)S(1)} collective-permute-done((bf16[1,256,1024]{2,1,0:T(8,128)(2,1)S(1)}, bf16[1,256,1024]{2,1,0:T(8,128)(2,1)S(1)}, u32[]{:S(2)}, u32[]{:S(2)}) %collective-permute-start.87) | collective-permute-done | bytes 524320 | tf_op jit(solution)/shard_map/ppermute | solution.py:30
  542.1 17.8 %collective-permute-done.73 = bf16[1,576,256]{2,1,0:T(8,128)(2,1)S(1)} collective-permute-done((bf16[1,576,256]{2,1,0:T(8,128)(2,1)S(1)}, bf16[1,576,256]{2,1,0:T(8,128)(2,1)S(1)}, u32[]{:S(2)}, u32[]{:S(2)}) %collective-permute-start.73) | collective-permute-done | bytes 294944 | tf_op jit(solution)/shard_map/ppermute | solution.py:30
  561.5 7.5 %collective-permute-done.75 = bf16[576,256]{1,0:T(8,128)(2,1)S(1)} collective-permute-done((bf16[576,256]{1,0:T(8,128)(2,1)S(1)}, bf16[576,256]{1,0:T(8,128)(2,1)S(1)}, u32[]{:S(2)}, u32[]{:S(2)}) %collective-permute-start.75) | collective-permute-done | bytes 294944 | tf_op jit(solution)/shard_map/ppermute | solution.py:30
  572.2 1.7 fusion.10
  (354 shorter events, 127.0 us)
Async XLA Ops:
  17.4 5.4 collective-permute-start.3
  25.4 5.5 collective-permute-start.6
  29.1 4.5 collective-permute-start.5
  29.1 4.5 collective-permute-start.4
  49.5 4.5 collective-permute-start.10
  55.1 5.5 collective-permute-start.13
  56.7 4.6 collective-permute-start.12
  77.3 4.9 collective-permute-start.17
  84.3 6.1 %collective-permute-start.20 = (f32[2,2,2048]{2,1,0:T(2,128)S(1)}, f32[2,2,2048]{2,1,0:T(2,128)S(1)}, u32[]{:S(2)}, u32[]{:S(2)}) collective-permute-start(f32[2,2,2048]{2,1,0:T(2,128)S(1)} %add_add_fusion.7), channel_id=1, source_target_pairs={{0,24},{1,25},{2,26},{3,27},{4,28},{5,29},{6,30},{7,31},{8,16},{9,... | collective-permute-start | bytes 98312 | tf_op jit(solution)/shard_map/ppermute | solution.py:30
  86.9 4.8 collective-permute-start.19
  118.0 4.9 collective-permute-start.24
  124.0 5.8 %collective-permute-start.27 = (f32[2,2,2048]{2,1,0:T(2,128)S(1)}, f32[2,2,2048]{2,1,0:T(2,128)S(1)}, u32[]{:S(2)}, u32[]{:S(2)}) collective-permute-start(f32[2,2,2048]{2,1,0:T(2,128)S(1)} %add_add_fusion.5), channel_id=1, source_target_pairs={{0,24},{1,25},{2,26},{3,27},{4,28},{5,29},{6,30},{7,31},{8,16},{9,... | collective-permute-start | bytes 98312 | tf_op jit(solution)/shard_map/ppermute | solution.py:30
  125.4 4.8 collective-permute-start.26
  134.0 5.9 %collective-permute-start.30 = (bf16[1,2,36,128]{3,2,1,0:T(8,128)(2,1)}, bf16[1,2,36,128]{3,2,1,0:T(8,128)(2,1)S(1)}, u32[]{:S(2)}, u32[]{:S(2)}) collective-permute-start(bf16[1,2,36,128]{3,2,1,0:T(8,128)(2,1)} %bitcast.235), channel_id=1, source_target_pairs={{0,24},{1,25},{2,26},{3,27},{4,28},{5,29},{6,30},{7,31},{8,16},{9,... | collective-permute-start | bytes 55304 | tf_op jit(solution)/shard_map/ppermute | solution.py:30
  136.4 5.0 collective-permute-start.29
  142.3 7.6 %collective-permute-start.33 = (bf16[4,2,36,128]{3,2,1,0:T(8,128)(2,1)S(1)}, bf16[4,2,36,128]{3,2,1,0:T(8,128)(2,1)S(1)}, u32[]{:S(2)}, u32[]{:S(2)}) collective-permute-start(bf16[4,2,36,128]{3,2,1,0:T(8,128)(2,1)S(1)} %pad_maximum_fusion), channel_id=1, source_target_pairs={{0,6},{1,7},{2,4},{3,5},{4,2},{5,3},{6,0},{7,1},{8,14},{9,15},{10,... | collective-permute-start | bytes 221192 | tf_op jit(solution)/shard_map/ppermute | solution.py:30
  144.8 5.0 collective-permute-start.32
  167.7 5.0 collective-permute-start.38
  173.7 5.8 %collective-permute-start.41 = (f32[2,2,2048]{2,1,0:T(2,128)S(1)}, f32[2,2,2048]{2,1,0:T(2,128)S(1)}, u32[]{:S(2)}, u32[]{:S(2)}) collective-permute-start(f32[2,2,2048]{2,1,0:T(2,128)S(1)} %add_add_fusion.3), channel_id=1, source_target_pairs={{0,24},{1,25},{2,26},{3,27},{4,28},{5,29},{6,30},{7,31},{8,16},{9,... | collective-permute-start | bytes 98312 | tf_op jit(solution)/shard_map/ppermute | solution.py:30
  175.2 4.8 collective-permute-start.40
  178.2 191.9 %collective-permute-start.91 = (bf16[8,256,64]{1,2,0:T(8,128)(2,1)S(1)}, bf16[8,256,64]{1,2,0:T(8,128)(2,1)S(1)}, u32[]{:S(2)}, u32[]{:S(2)}) collective-permute-start(bf16[8,256,64]{1,2,0:T(8,128)(2,1)S(1)} %broadcast_select_fusion.4), channel_id=1, source_target_pairs={{0,1},{1,0},{2,3},{3,2},{4,5},{5,4},{6,7},{7,6},{8,9},{9,8},{10,11... | collective-permute-start | bytes 786440 | tf_op jit(solution)/shard_map/ppermute | solution.py:30
  214.6 5.8 %collective-permute-start.45 = (f32[2,2,2048]{2,1,0:T(2,128)S(1)}, f32[2,2,2048]{2,1,0:T(2,128)S(1)}, u32[]{:S(2)}, u32[]{:S(2)}) collective-permute-start(f32[2,2,2048]{2,1,0:T(2,128)S(1)} %add.376), channel_id=1, source_target_pairs={{0,6},{1,7},{2,4},{3,5},{4,2},{5,3},{6,0},{7,1},{8,14},{9,15},{10,... | collective-permute-start | bytes 98312 | tf_op jit(solution)/shard_map/ppermute | solution.py:30
  221.6 5.9 %collective-permute-start.48 = (f32[2,2,2048]{2,1,0:T(2,128)S(1)}, f32[2,2,2048]{2,1,0:T(2,128)S(1)}, u32[]{:S(2)}, u32[]{:S(2)}) collective-permute-start(f32[2,2,2048]{2,1,0:T(2,128)S(1)} %add_add_fusion.1), channel_id=1, source_target_pairs={{0,24},{1,25},{2,26},{3,27},{4,28},{5,29},{6,30},{7,31},{8,16},{9,... | collective-permute-start | bytes 98312 | tf_op jit(solution)/shard_map/ppermute | solution.py:30
  224.1 4.9 collective-permute-start.47
  226.7 189.4 %collective-permute-start.84 = (bf16[8,256,1024]{2,1,0:T(8,128)(2,1)}, bf16[8,256,1024]{2,1,0:T(8,128)(2,1)}, u32[]{:S(2)}, u32[]{:S(2)}) collective-permute-start(bf16[8,256,1024]{2,1,0:T(8,128)(2,1)} %broadcast_select_fusion), channel_id=1, source_target_pairs={{0,1},{1,0},{2,3},{3,2},{4,5},{5,4},{6,7},{7,6},{8,9},{9,8},{10,11... | collective-permute-start | bytes 12582920 | tf_op jit(solution)/shard_map/ppermute | solution.py:30
  250.5 7.9 %collective-permute-start.49 = (f32[2,2,512]{2,1,0:T(2,128)}, f32[2,2,512]{2,1,0:T(2,128)S(1)}, u32[]{:S(2)}, u32[]{:S(2)}) collective-permute-start(f32[2,2,512]{2,1,0:T(2,128)} %get-tuple-element.60), channel_id=1, source_target_pairs={{0,1},{1,0},{2,3},{3,2},{4,5},{5,4},{6,7},{7,6},{8,9},{9,8},{10,11... | collective-permute-start | bytes 24584 | tf_op jit(solution)/shard_map/ppermute | solution.py:30
  258.8 4.6 collective-permute-start.52
  264.4 5.5 collective-permute-start.55
  266.1 4.5 collective-permute-start.54
  288.5 33.2 %collective-permute-start.56 = (f32[2,2,512]{2,1,0:T(2,128)}, f32[2,2,512]{2,1,0:T(2,128)S(1)}, u32[]{:S(2)}, u32[]{:S(2)}) collective-permute-start(f32[2,2,512]{2,1,0:T(2,128)} %get-tuple-element.62), channel_id=1, source_target_pairs={{0,1},{1,0},{2,3},{3,2},{4,5},{5,4},{6,7},{7,6},{8,9},{9,8},{10,11... | collective-permute-start | bytes 24584 | tf_op jit(solution)/shard_map/ppermute | solution.py:30
  322.2 4.5 collective-permute-start.59
  328.8 6.1 %collective-permute-start.62 = (f32[2,2,512]{2,1,0:T(2,128)S(1)}, f32[2,2,512]{2,1,0:T(2,128)S(1)}, u32[]{:S(2)}, u32[]{:S(2)}) collective-permute-start(f32[2,2,512]{2,1,0:T(2,128)S(1)} %add_add_fusion.9), channel_id=1, source_target_pairs={{0,24},{1,25},{2,26},{3,27},{4,28},{5,29},{6,30},{7,31},{8,16},{9,... | collective-permute-start | bytes 24584 | tf_op jit(solution)/shard_map/ppermute | solution.py:30
  331.2 4.5 collective-permute-start.61
  334.9 76.1 %collective-permute-start.77 = (bf16[8,64,1024]{2,1,0:T(8,128)(2,1)}, bf16[8,64,1024]{2,1,0:T(8,128)(2,1)}, u32[]{:S(2)}, u32[]{:S(2)}) collective-permute-start(bf16[8,64,1024]{2,1,0:T(8,128)(2,1)} %broadcast_select_fusion.2), channel_id=1, source_target_pairs={{0,1},{1,0},{2,3},{3,2},{4,5},{5,4},{6,7},{7,6},{8,9},{9,8},{10,11... | collective-permute-start | bytes 3145736 | tf_op jit(solution)/shard_map/ppermute | solution.py:30
  370.3 5.0 collective-permute-start.92
  375.3 4.6 collective-permute-start.93
  376.4 5.7 collective-permute-start.95
  378.8 4.8 collective-permute-start.94
  380.0 35.1 %collective-permute-start.63 = (bf16[8,256,256]{2,1,0:T(8,128)(2,1)}, bf16[8,256,256]{2,1,0:T(8,128)(2,1)S(1)}, u32[]{:S(2)}, u32[]{:S(2)}) collective-permute-start(bf16[8,256,256]{2,1,0:T(8,128)(2,1)} %broadcast_select_fusion.3), channel_id=1, source_target_pairs={{0,1},{1,0},{2,3},{3,2},{4,5},{5,4},{6,7},{7,6},{8,9},{9,8},{10,11... | collective-permute-start | bytes 3145736 | tf_op jit(solution)/shard_map/ppermute | solution.py:30
  384.8 55.3 %collective-permute-start.70 = (bf16[8,576,256]{2,1,0:T(8,128)(2,1)}, bf16[8,576,256]{2,1,0:T(8,128)(2,1)}, u32[]{:S(2)}, u32[]{:S(2)}) collective-permute-start(bf16[8,576,256]{2,1,0:T(8,128)(2,1)} %broadcast_select_fusion.1), channel_id=1, source_target_pairs={{0,1},{1,0},{2,3},{3,2},{4,5},{5,4},{6,7},{7,6},{8,9},{9,8},{10,11... | collective-permute-start | bytes 7077896 | tf_op jit(solution)/shard_map/ppermute | solution.py:30
  387.6 22.6 %collective-permute-start.97 = (bf16[256,64]{0,1:T(8,128)(2,1)S(1)}, bf16[256,64]{0,1:T(8,128)(2,1)S(1)}, u32[]{:S(2)}, u32[]{:S(2)}) collective-permute-start(bf16[256,64]{0,1:T(8,128)(2,1)S(1)} %add_convert_fusion.9), channel_id=1, source_target_pairs={{0,1},{1,0},{2,3},{3,2},{4,5},{5,4},{6,7},{7,6},{8,9},{9,8},{10,11... | collective-permute-start | bytes 98312 | tf_op jit(solution)/shard_map/ppermute | solution.py:30
  413.5 14.8 %collective-permute-start.78 = (bf16[4,64,1024]{2,1,0:T(8,128)(2,1)S(1)}, bf16[4,64,1024]{2,1,0:T(8,128)(2,1)S(1)}, u32[]{:S(2)}, u32[]{:S(2)}) collective-permute-start(bf16[4,64,1024]{2,1,0:T(8,128)(2,1)S(1)} %slice_bitcast_fusion.8), channel_id=1, source_target_pairs={{0,4},{1,5},{2,6},{3,7},{4,0},{5,1},{6,2},{7,3},{8,12},{9,13},{10,... | collective-permute-start | bytes 1572872 | tf_op jit(solution)/shard_map/ppermute | solution.py:30
  415.5 24.0 %collective-permute-start.64 = (bf16[4,256,256]{2,1,0:T(8,128)(2,1)S(1)}, bf16[4,256,256]{2,1,0:T(8,128)(2,1)S(1)}, u32[]{:S(2)}, u32[]{:S(2)}) collective-permute-start(bf16[4,256,256]{2,1,0:T(8,128)(2,1)S(1)} %slice_bitcast_fusion.10), channel_id=1, source_target_pairs={{0,4},{1,5},{2,6},{3,7},{4,0},{5,1},{6,2},{7,3},{8,12},{9,13},{10,... | collective-permute-start | bytes 1572872 | tf_op jit(solution)/shard_map/ppermute | solution.py:30
  423.1 61.4 %collective-permute-start.85 = (bf16[4,256,1024]{2,1,0:T(8,128)(2,1)S(1)}, bf16[4,256,1024]{2,1,0:T(8,128)(2,1)S(1)}, u32[]{:S(2)}, u32[]{:S(2)}) collective-permute-start(bf16[4,256,1024]{2,1,0:T(8,128)(2,1)S(1)} %slice_bitcast_fusion), channel_id=1, source_target_pairs={{0,4},{1,5},{2,6},{3,7},{4,0},{5,1},{6,2},{7,3},{8,12},{9,13},{10,... | collective-permute-start | bytes 6291464 | tf_op jit(solution)/shard_map/ppermute | solution.py:30
  428.6 15.9 %collective-permute-start.79 = (bf16[1,64,1024]{2,1,0:T(8,128)(2,1)S(1)}, bf16[1,64,1024]{2,1,0:T(8,128)(2,1)S(1)}, u32[]{:S(2)}, u32[]{:S(2)}) collective-permute-start(bf16[1,64,1024]{2,1,0:T(8,128)(2,1)S(1)} %get-tuple-element.144), channel_id=1, source_target_pairs={{0,8},{1,9},{2,10},{3,11},{4,12},{5,13},{6,14},{7,15},{8,0},{9,1},... | collective-permute-start | bytes 393224 | tf_op jit(solution)/shard_map/ppermute | solution.py:30
  428.7 17.7 %collective-permute-start.81 = (bf16[1,64,1024]{2,1,0:T(8,128)(2,1)S(1)}, bf16[1,64,1024]{2,1,0:T(8,128)(2,1)S(1)}, u32[]{:S(2)}, u32[]{:S(2)}) collective-permute-start(bf16[1,64,1024]{2,1,0:T(8,128)(2,1)S(1)} %get-tuple-element.145), channel_id=1, source_target_pairs={{0,24},{1,25},{2,26},{3,27},{4,28},{5,29},{6,30},{7,31},{8,16},{9,... | collective-permute-start | bytes 393224 | tf_op jit(solution)/shard_map/ppermute | solution.py:30
  439.6 9.0 %collective-permute-start.80 = (bf16[1,64,1024]{2,1,0:T(8,128)(2,1)S(1)}, bf16[1,64,1024]{2,1,0:T(8,128)(2,1)S(1)}, u32[]{:S(2)}, u32[]{:S(2)}) collective-permute-start(bf16[1,64,1024]{2,1,0:T(8,128)(2,1)S(1)} %get-tuple-element.146), channel_id=1, source_target_pairs={{0,16},{1,17},{2,18},{3,19},{4,20},{5,21},{6,22},{7,23},{8,24},{9,... | collective-permute-start | bytes 393224 | tf_op jit(solution)/shard_map/ppermute | solution.py:30
  442.9 66.5 %collective-permute-start.71 = (bf16[4,576,256]{2,1,0:T(8,128)(2,1)S(1)}, bf16[4,576,256]{2,1,0:T(8,128)(2,1)S(1)}, u32[]{:S(2)}, u32[]{:S(2)}) collective-permute-start(bf16[4,576,256]{2,1,0:T(8,128)(2,1)S(1)} %slice_bitcast_fusion.2), channel_id=1, source_target_pairs={{0,4},{1,5},{2,6},{3,7},{4,0},{5,1},{6,2},{7,3},{8,12},{9,13},{10,... | collective-permute-start | bytes 3538952 | tf_op jit(solution)/shard_map/ppermute | solution.py:30
  444.5 7.5 %collective-permute-start.65 = (bf16[1,256,256]{2,1,0:T(8,128)(2,1)S(1)}, bf16[1,256,256]{2,1,0:T(8,128)(2,1)S(1)}, u32[]{:S(2)}, u32[]{:S(2)}) collective-permute-start(bf16[1,256,256]{2,1,0:T(8,128)(2,1)S(1)} %get-tuple-element.147), channel_id=1, source_target_pairs={{0,8},{1,9},{2,10},{3,11},{4,12},{5,13},{6,14},{7,15},{8,0},{9,1},... | collective-permute-start | bytes 393224 | tf_op jit(solution)/shard_map/ppermute | solution.py:30
  446.4 8.6 %collective-permute-start.67 = (bf16[1,256,256]{2,1,0:T(8,128)(2,1)S(1)}, bf16[1,256,256]{2,1,0:T(8,128)(2,1)S(1)}, u32[]{:S(2)}, u32[]{:S(2)}) collective-permute-start(bf16[1,256,256]{2,1,0:T(8,128)(2,1)S(1)} %get-tuple-element.148), channel_id=1, source_target_pairs={{0,24},{1,25},{2,26},{3,27},{4,28},{5,29},{6,30},{7,31},{8,16},{9,... | collective-permute-start | bytes 393224 | tf_op jit(solution)/shard_map/ppermute | solution.py:30
  448.6 10.5 %collective-permute-start.66 = (bf16[1,256,256]{2,1,0:T(8,128)(2,1)S(1)}, bf16[1,256,256]{2,1,0:T(8,128)(2,1)S(1)}, u32[]{:S(2)}, u32[]{:S(2)}) collective-permute-start(bf16[1,256,256]{2,1,0:T(8,128)(2,1)S(1)} %get-tuple-element.149), channel_id=1, source_target_pairs={{0,16},{1,17},{2,18},{3,19},{4,20},{5,21},{6,22},{7,23},{8,24},{9,... | collective-permute-start | bytes 393224 | tf_op jit(solution)/shard_map/ppermute | solution.py:30
  452.0 89.4 %collective-permute-start.82 = (bf16[64,1024]{1,0:T(8,128)(2,1)S(1)}, bf16[64,1024]{1,0:T(8,128)(2,1)S(1)}, u32[]{:S(2)}, u32[]{:S(2)}) collective-permute-start(bf16[64,1024]{1,0:T(8,128)(2,1)S(1)} %fusion.35), channel_id=1, source_target_pairs={{0,2},{1,3},{2,0},{3,1},{4,6},{5,7},{6,4},{7,5},{8,10},{9,11},{10,... | collective-permute-start | bytes 393224 | tf_op jit(solution)/shard_map/ppermute | solution.py:30
  459.2 101.4 %collective-permute-start.68 = (bf16[256,256]{1,0:T(8,128)(2,1)S(1)}, bf16[256,256]{1,0:T(8,128)(2,1)S(1)}, u32[]{:S(2)}, u32[]{:S(2)}) collective-permute-start(bf16[256,256]{1,0:T(8,128)(2,1)S(1)} %fusion.34), channel_id=1, source_target_pairs={{0,2},{1,3},{2,0},{3,1},{4,6},{5,7},{6,4},{7,5},{8,10},{9,11},{10,... | collective-permute-start | bytes 393224 | tf_op jit(solution)/shard_map/ppermute | solution.py:30
  485.7 24.5 %collective-permute-start.86 = (bf16[1,256,1024]{2,1,0:T(8,128)(2,1)S(1)}, bf16[1,256,1024]{2,1,0:T(8,128)(2,1)S(1)}, u32[]{:S(2)}, u32[]{:S(2)}) collective-permute-start(bf16[1,256,1024]{2,1,0:T(8,128)(2,1)S(1)} %get-tuple-element.130), channel_id=1, source_target_pairs={{0,8},{1,9},{2,10},{3,11},{4,12},{5,13},{6,14},{7,15},{8,0},{9,1},... | collective-permute-start | bytes 1572872 | tf_op jit(solution)/shard_map/ppermute | solution.py:30
  485.8 26.2 %collective-permute-start.88 = (bf16[1,256,1024]{2,1,0:T(8,128)(2,1)S(1)}, bf16[1,256,1024]{2,1,0:T(8,128)(2,1)S(1)}, u32[]{:S(2)}, u32[]{:S(2)}) collective-permute-start(bf16[1,256,1024]{2,1,0:T(8,128)(2,1)S(1)} %get-tuple-element.131), channel_id=1, source_target_pairs={{0,24},{1,25},{2,26},{3,27},{4,28},{5,29},{6,30},{7,31},{8,16},{9,... | collective-permute-start | bytes 1572872 | tf_op jit(solution)/shard_map/ppermute | solution.py:30
  509.4 31.6 %collective-permute-start.87 = (bf16[1,256,1024]{2,1,0:T(8,128)(2,1)S(1)}, bf16[1,256,1024]{2,1,0:T(8,128)(2,1)S(1)}, u32[]{:S(2)}, u32[]{:S(2)}) collective-permute-start(bf16[1,256,1024]{2,1,0:T(8,128)(2,1)S(1)} %get-tuple-element.132), channel_id=1, source_target_pairs={{0,16},{1,17},{2,18},{3,19},{4,20},{5,21},{6,22},{7,23},{8,24},{9,... | collective-permute-start | bytes 1572872 | tf_op jit(solution)/shard_map/ppermute | solution.py:30
  510.2 31.8 %collective-permute-start.72 = (bf16[1,576,256]{2,1,0:T(8,128)(2,1)S(1)}, bf16[1,576,256]{2,1,0:T(8,128)(2,1)S(1)}, u32[]{:S(2)}, u32[]{:S(2)}) collective-permute-start(bf16[1,576,256]{2,1,0:T(8,128)(2,1)S(1)} %get-tuple-element.133), channel_id=1, source_target_pairs={{0,8},{1,9},{2,10},{3,11},{4,12},{5,13},{6,14},{7,15},{8,0},{9,1},... | collective-permute-start | bytes 884744 | tf_op jit(solution)/shard_map/ppermute | solution.py:30
  512.0 30.0 %collective-permute-start.74 = (bf16[1,576,256]{2,1,0:T(8,128)(2,1)S(1)}, bf16[1,576,256]{2,1,0:T(8,128)(2,1)S(1)}, u32[]{:S(2)}, u32[]{:S(2)}) collective-permute-start(bf16[1,576,256]{2,1,0:T(8,128)(2,1)S(1)} %get-tuple-element.134), channel_id=1, source_target_pairs={{0,24},{1,25},{2,26},{3,27},{4,28},{5,29},{6,30},{7,31},{8,16},{9,... | collective-permute-start | bytes 884744 | tf_op jit(solution)/shard_map/ppermute | solution.py:30
  541.0 18.9 %collective-permute-start.73 = (bf16[1,576,256]{2,1,0:T(8,128)(2,1)S(1)}, bf16[1,576,256]{2,1,0:T(8,128)(2,1)S(1)}, u32[]{:S(2)}, u32[]{:S(2)}) collective-permute-start(bf16[1,576,256]{2,1,0:T(8,128)(2,1)S(1)} %get-tuple-element.135), channel_id=1, source_target_pairs={{0,16},{1,17},{2,18},{3,19},{4,20},{5,21},{6,22},{7,23},{8,24},{9,... | collective-permute-start | bytes 884744 | tf_op jit(solution)/shard_map/ppermute | solution.py:30
  541.4 19.4 %collective-permute-start.89 = (bf16[256,1024]{1,0:T(8,128)(2,1)S(1)}, bf16[256,1024]{1,0:T(8,128)(2,1)S(1)}, u32[]{:S(2)}, u32[]{:S(2)}) collective-permute-start(bf16[256,1024]{1,0:T(8,128)(2,1)S(1)} %fusion.22), channel_id=1, source_target_pairs={{0,2},{1,3},{2,0},{3,1},{4,6},{5,7},{6,4},{7,5},{8,10},{9,11},{10,... | collective-permute-start | bytes 1572872 | tf_op jit(solution)/shard_map/ppermute | solution.py:30
  542.0 27.2 %collective-permute-start.83 = (bf16[64,1024]{1,0:T(8,128)(2,1)S(1)}, bf16[64,1024]{1,0:T(8,128)(2,1)S(1)}, u32[]{:S(2)}, u32[]{:S(2)}) collective-permute-start(bf16[64,1024]{1,0:T(8,128)(2,1)S(1)} %add_convert_fusion.7), channel_id=1, source_target_pairs={{0,1},{1,0},{2,3},{3,2},{4,5},{5,4},{6,7},{7,6},{8,9},{9,8},{10,11... | collective-permute-start | bytes 393224 | tf_op jit(solution)/shard_map/ppermute | solution.py:30
  560.0 9.0 %collective-permute-start.75 = (bf16[576,256]{1,0:T(8,128)(2,1)S(1)}, bf16[576,256]{1,0:T(8,128)(2,1)S(1)}, u32[]{:S(2)}, u32[]{:S(2)}) collective-permute-start(bf16[576,256]{1,0:T(8,128)(2,1)S(1)} %fusion.24), channel_id=1, source_target_pairs={{0,2},{1,3},{2,0},{3,1},{4,6},{5,7},{6,4},{7,5},{8,10},{9,11},{10,... | collective-permute-start | bytes 884744 | tf_op jit(solution)/shard_map/ppermute | solution.py:30
  560.6 9.4 %collective-permute-start.69 = (bf16[256,256]{1,0:T(8,128)(2,1)S(1)}, bf16[256,256]{1,0:T(8,128)(2,1)S(1)}, u32[]{:S(2)}, u32[]{:S(2)}) collective-permute-start(bf16[256,256]{1,0:T(8,128)(2,1)S(1)} %add_convert_fusion.8), channel_id=1, source_target_pairs={{0,1},{1,0},{2,3},{3,2},{4,5},{5,4},{6,7},{7,6},{8,9},{9,8},{10,11... | collective-permute-start | bytes 393224 | tf_op jit(solution)/shard_map/ppermute | solution.py:30
  560.9 11.3 %collective-permute-start.90 = (bf16[256,1024]{1,0:T(8,128)(2,1)S(1)}, bf16[256,1024]{1,0:T(8,128)(2,1)S(1)}, u32[]{:S(2)}, u32[]{:S(2)}) collective-permute-start(bf16[256,1024]{1,0:T(8,128)(2,1)S(1)} %add_convert_fusion.4), channel_id=1, source_target_pairs={{0,1},{1,0},{2,3},{3,2},{4,5},{5,4},{6,7},{7,6},{8,9},{9,8},{10,11... | collective-permute-start | bytes 1572872 | tf_op jit(solution)/shard_map/ppermute | solution.py:30
  (57 other events, 422.4 us)
